TPU v7x, 32 devices: a whole 2x2x4 slice. The times are simulated.
32 devices in a mesh: dp: 8 (over z, x), mp: 4 (over y, core).
Axes of the slice: x: 2, y: 2, z: 4, core: 2. Of those that a mesh axis runs over, the one named last changes fastest.
Arguments:
- inputs: bfloat16 [32, 1024, 512], P('dp', None, 'mp'), may hold values from -6 to 6
- cotangent: bfloat16 [32, 1024, 512], P('dp', None, 'mp'), may hold values from -6 to 6
- lengths: int32 [32], P('dp'), may hold values from 256 to 1024, as said below
- conv_master: float32 [9, 512, 512], P(None, 'dp', 'mp'), may hold values from -0.09375 to 0.09375
- hidden_master: float32 [512, 2048], P('dp', 'mp'), may hold values from -0.25 to 0.25
- output_master: float32 [2048, 512], P('mp', 'dp'), may hold values from -0.125 to 0.125
- conv_first: float32 [9, 512, 512], P(None, 'dp', 'mp'), may hold values from -0.00030517578 to 0.00030517578
- hidden_first: float32 [512, 2048], P('dp', 'mp'), may hold values from -0.00030517578 to 0.00030517578
- output_first: float32 [2048, 512], P('mp', 'dp'), may hold values from -0.00030517578 to 0.00030517578
- conv_second: float32 [9, 512, 512], P(None, 'dp', 'mp'), may hold values from 2.2413645e-10 to 8.965458e-10
- hidden_second: float32 [512, 2048], P('dp', 'mp'), may hold values from 2.2413645e-10 to 8.965458e-10
- output_second: float32 [2048, 512], P('mp', 'dp'), may hold values from 2.2413645e-10 to 8.965458e-10
- vectors: float32 [6, 512], replicated, may hold values from -0.6 to 6.5, as said below
- vector_first: float32 [6, 512], replicated, may hold values from -0.00024414062 to 0.00024414062
- vector_second: float32 [6, 512], replicated, may hold values from 1.1206822e-10 to 4.482729e-10
- hidden_bias: float32 [2048], P('mp'), may hold values from -3 to 3
- bias_first: float32 [2048], P('mp'), may hold values from -0.00010681152 to 0.00010681152
- bias_second: float32 [2048], P('mp'), may hold values from 2.2413644e-11 to 8.9654575e-11
Outputs:
- block_output: bfloat16 [32, 1024, 512], P('dp', None, 'mp')
- input_grad: float32 [32, 1024, 512], P('dp', None, 'mp')
- grad_norm: float32 [], replicated
- conv_weight_new: float32 [9, 512, 512], P(None, 'dp', 'mp')
- conv_first_new: float32 [9, 512, 512], P(None, 'dp', 'mp')
- conv_second_new: float32 [9, 512, 512], P(None, 'dp', 'mp')
- hidden_weight_new: float32 [512, 2048], P('dp', 'mp')
- hidden_first_new: float32 [512, 2048], P('dp', 'mp')
- hidden_second_new: float32 [512, 2048], P('dp', 'mp')
- output_weight_new: float32 [2048, 512], P('mp', 'dp')
- output_first_new: float32 [2048, 512], P('mp', 'dp')
- output_second_new: float32 [2048, 512], P('mp', 'dp')
- vectors_new: float32 [6, 512], replicated
- vector_first_new: float32 [6, 512], replicated
- vector_second_new: float32 [6, 512], replicated
- hidden_bias_new: float32 [2048], P('mp')
- bias_first_new: float32 [2048], P('mp')
- bias_second_new: float32 [2048], P('mp')
Inputs may be any that keep to these rules, and one draw needn't show every extreme that they name: `lengths`: each window's valid length is 256, 512 or 1024; the first window has 256 and the last 1024. `vectors`: gains are positive.
All inputs are finite; a program needn't handle non-finite values.
Results may differ from a plain program's by a relative error of at most 0.0095.
Values may be sent and summed in bfloat16 or wider, within the bound.
No kernel may reach another device: no remote copies, remote signals or barrier semaphores. Data moves between devices by JAX's collectives and lax.ppermute only.
A program may use at most 192 MiB of HBM per device.

v0:
```python
import functools

import jax
import jax.numpy as jnp
from jax import lax
from jax.experimental import pallas as pl
from jax.experimental.pallas import tpu as pltpu
from jax.sharding import PartitionSpec as P

KERNEL = 9
DILATION = 8
REACH = DILATION * (KERNEL // 2)
STEP = 10
ROWS = 256

NORM_EPS = 1e-05
BETA_ONE = 0.9
BETA_TWO = 0.999
ADAM_EPS = 1e-08
MATRIX_RATE = 0.03
VECTOR_RATE = 0.3
WEIGHT_DECAY = 0.01
CLIP_NORM = 1.0

f32 = jnp.float32
bf16 = jnp.bfloat16
NN = (((1,), (0,)), ((), ()))
NT = (((1,), (1,)), ((), ()))


def dot(a, b, dims=NN):
    return lax.dot_general(a, b, dims, preferred_element_type=f32)


def phi_of(v):
    return 0.5 * (1.0 + lax.erf(v * 0.7071067811865476))


def slope_of(v, phi):
    return phi + v * jnp.exp(-0.5 * v * v) * 0.3989422804014327


def norm_parts(v):
    centre = v - jnp.mean(v, axis=-1, keepdims=True)
    inverse = lax.rsqrt(jnp.mean(centre * centre, axis=-1, keepdims=True) + NORM_EPS)
    return centre * inverse, inverse


def norm_back(e, s, inverse):
    return inverse * (
        e - jnp.mean(e, axis=-1, keepdims=True) - s * jnp.mean(e * s, axis=-1, keepdims=True)
    )


def source_of(place, dc, b, a, dz):
    dp, mp = place[0], place[1]
    flip = (mp & 1) ^ dc
    fx = jnp.where(flip == 0, a, b)
    fy = jnp.where(flip == 0, b, a)
    d = ((dp >> 1) ^ dz) * 2 + ((dp & 1) ^ fx)
    m = ((mp >> 1) ^ fy) * 2 + ((mp & 1) ^ dc)
    return d, m


def share_index(place, d, parity, j):
    dp, mp = place[0], place[1]
    fx = (dp & 1) ^ (d & 1)
    fy = (mp >> 1) ^ j
    odd = parity == 1
    return jnp.where(odd, fx, fy), jnp.where(odd, fy, fx), (dp >> 1) ^ (d >> 1)


def store_columns(place, outs, rows, values):
    for k, out in enumerate(outs):
        own = out.shape[1]
        out[rows, :] = values[:, pl.ds(mult((place[1] ^ k) * own, own), own)]


def mult(v, n):
    return v if isinstance(v, int) else pl.multiple_of(v, n)


def put_shifted(pair, last, row, values):
    count = values.shape[0]
    pair[0, pl.ds(mult(row + REACH, 16), count), :] = values.astype(bf16)
    moved = jnp.concatenate([last[...], values[: count - DILATION]])
    pair[1, pl.ds(mult(row + REACH - 2 * DILATION, 16), count), :] = moved.astype(bf16)
    last[...] = values[count - DILATION :]


def clear_shifted(pair, last):
    width = pair.shape[2]
    pair[0, 0:REACH, :] = jnp.zeros((REACH, width), bf16)
    pair[1, 0 : REACH - 2 * DILATION, :] = jnp.zeros((REACH - 2 * DILATION, width), bf16)
    last[...] = jnp.zeros_like(last)


def end_shifted(pair, last, length, blocks, most):
    width = pair.shape[2]
    tail = jnp.concatenate([last[...], jnp.zeros_like(last)]).astype(bf16)
    pair[1, pl.ds(mult(length + REACH - 2 * DILATION, 16), 2 * DILATION), :] = tail

    def clear(i, _):
        for j in (0, 1):
            rows = pl.ds(mult(i * ROWS + REACH, 16), ROWS)
            pair[j, rows, :] = jnp.zeros((ROWS, width), bf16)
        return 0

    lax.fori_loop(blocks, most, clear, 0)
    for j in (0, 1):
        pair[j, most * ROWS + REACH :, :] = jnp.zeros((REACH, width), bf16)


SLOTS = tuple((dc, b, a) for dc in (0, 1) for b, a in ((0, 0), (0, 1), (1, 0), (1, 1)))


def fetch_rows(place, parts, whole, sems):
    seq, own = whole.shape[0], parts[0].shape[1]
    copies = []
    for k, part in enumerate(parts):
        target = whole.at[:, pl.ds(mult((place[1] ^ k) * own, own), own)]
        copies.append(pltpu.make_async_copy(part.at[pl.ds(0, seq), :], target, sems.at[k]))
        copies[-1].start()
    return copies


def fetch_shards(shards, sems):
    copies = []
    for index, shard, whole, d, m in shards:
        di, cols = shard.shape[-2:]
        target = whole.at[
            (slice(None),) * (len(shard.shape) - 2)
            + (pl.ds(mult(d * di, di), di), pl.ds(mult(m * cols, cols), cols))
        ]
        copies.append(pltpu.make_async_copy(shard, target, sems.at[index]))
        copies[-1].start()
    return copies


def conv_forward(place, x0, x1, x2, x3, vec, *rest):
    pieces = rest[:8]
    w_out, x_out, na_out, resid, slope, bias_out, nab, last, whole, extra, sems, x_sem = rest[8:]
    full = vec.shape[1]
    seq, own = x_out.shape[0], x0.shape[1]
    length, blocks = place[2:]

    x_parts = (x0, x1, x2, x3)
    rows = fetch_rows(place, x_parts, x_out, x_sem.at[0])
    shards = fetch_shards(
        [
            ((slot, z), piece.at[z], whole, *source_of(place, *index, z))
            for slot, (index, piece) in enumerate(zip(SLOTS, pieces))
            for z in range(piece.shape[0])
        ],
        sems,
    )
    extras = [
        pltpu.make_async_copy(part.at[pl.ds(seq, extra.shape[1]), :], extra.at[k], x_sem.at[1, k])
        for k, part in enumerate(x_parts)
    ]
    for copy in extras:
        copy.start()
    for copy in rows + extras:
        copy.wait()
    for k in range(len(x_parts)):
        values = extra[k].astype(f32)
        units = values.shape[0] // 4
        bias_out[place[1] ^ k] = (values[0:units] + values[units : 2 * units]) + values[
            2 * units : 3 * units
        ]

    gain = vec[0:1, :]
    shift = vec[1:2, :]
    clear_shifted(nab, last)

    def norm_step(i, _):
        row = mult(i * ROWS, ROWS)
        rows = pl.ds(row, ROWS)
        scaled, _ = norm_parts(x_out[rows, :].astype(f32))
        values = scaled * gain + shift
        put_shifted(nab, last, row, values)
        na_out[rows, :] = values.astype(bf16)
        return 0

    def idle_step(i, _):
        na_out[pl.ds(mult(i * ROWS, ROWS), ROWS), :] = jnp.zeros((ROWS, full), bf16)
        return 0

    lax.fori_loop(0, blocks, norm_step, 0)
    lax.fori_loop(blocks, seq // ROWS, idle_step, 0)
    end_shifted(nab, last, length, blocks, seq // ROWS)
    for copy in shards:
        copy.wait()
    w_copy = pltpu.make_async_copy(whole, w_out, x_sem.at[2, 0])
    w_copy.start()

    def conv_step(i, _):
        row = mult(i * ROWS, ROWS)
        window = jnp.concatenate(
            [
                nab[t & 1, pl.ds(mult(row + DILATION * (t - (t & 1)), 16), ROWS), :]
                for t in range(KERNEL)
            ],
            axis=1,
        )
        weights = whole[...].reshape(KERNEL * full, full)
        rows = pl.ds(row, ROWS)
        conv = dot(window, weights) + vec[2:3, :]
        phi = phi_of(conv)
        resid[rows, :] = x_out[rows, :].astype(f32) + conv * phi
        slope[rows, :] = slope_of(conv, phi)
        return 0

    lax.fori_loop(0, blocks, conv_step, 0)
    w_copy.wait()


def ffn_hidden(place, x_full, resid, c0, c1, c2, c3, vec, hbias, *rest):
    pieces = rest[:8]
    outs, (act, hg, sec, mg, wh_out) = rest[8:12], rest[12:17]
    whole, values_ref, sems, c_sem = rest[17:]
    wh, wo = whole.at[0], whole.at[1]
    seq, full = x_full.shape
    hidden = hbias.shape[1]
    blocks = place[3]

    rows = fetch_rows(place, (c0, c1, c2, c3), mg, c_sem.at[0])
    shards = []
    for slot, piece in enumerate(pieces):
        w, dc, dx = slot >> 2, (slot >> 1) & 1, slot & 1
        for z in range(piece.shape[0]):
            for dy in (0, 1):
                d = ((place[0] >> 1) ^ z) * 2 + ((place[0] & 1) ^ dx)
                m = place[1] ^ (dy * 2 + dc)
                shards.append(((slot, z, dy), piece.at[z, dy], whole.at[w], d, m))
    shards = fetch_shards(shards, sems)
    for copy in rows + shards:
        copy.wait()
    wh_copy = pltpu.make_async_copy(wh, wh_out, c_sem.at[1, 0])
    wh_copy.start()

    def row_step(i, _):
        rows = pl.ds(mult(i * ROWS, ROWS), ROWS)
        residual = resid[rows, :]
        s, _ = norm_parts(residual)
        second = (s * vec[3:4, :] + vec[4:5, :]).astype(bf16)
        sec[rows, :] = second
        grad = mg[rows, :]
        for j in range(hidden // 512):
            cols = slice(j * 512, (j + 1) * 512)
            h = dot(second, wh[:, cols]) + hbias[0:1, cols]
            phi = phi_of(h)
            act[rows, cols] = (h * phi).astype(bf16)
            hidden_grad = (dot(grad, wo[:, cols]) * slope_of(h, phi)).astype(bf16)
            hg[rows, cols] = hidden_grad
        mixed = dot(act[rows, :], wo[...], NT)
        values_ref[...] = (residual + (mixed + vec[5:6, :])).astype(bf16)
        store_columns(place, outs, rows, values_ref)
        return 0

    def idle_step(i, _):
        rows = pl.ds(mult(i * ROWS, ROWS), ROWS)
        values_ref[...] = x_full[rows, :]
        store_columns(place, outs, rows, values_ref)
        sec[rows, :] = jnp.zeros((ROWS, full), bf16)
        for ref in (act, hg):
            ref[rows, :] = jnp.zeros((ROWS, hidden), bf16)
        return 0

    lax.fori_loop(0, blocks, row_step, 0)
    lax.fori_loop(blocks, seq // ROWS, idle_step, 0)
    wh_copy.wait()


def norm_backward(place, resid, slope, grad, hg, wh, vec, resid_out, cab, vgrad, last):
    seq = resid.shape[0]
    length, blocks = place[2:]
    vgrad[...] = jnp.zeros_like(vgrad)
    clear_shifted(cab, last)

    def row_step(i, _):
        row = mult(i * ROWS, ROWS)
        rows = pl.ds(row, ROWS)
        second_grad = dot(hg[rows, :], wh[...], NT)
        s, inverse = norm_parts(resid[rows, :])
        up = grad[rows, :].astype(f32)
        vgrad[3:4, :] += jnp.sum(second_grad * s, axis=0, keepdims=True)
        vgrad[4:5, :] += jnp.sum(second_grad, axis=0, keepdims=True)
        vgrad[5:6, :] += jnp.sum(up, axis=0, keepdims=True)
        resid_grad = up + norm_back(second_grad * vec[3:4, :], s, inverse)
        resid_out[rows, :] = resid_grad
        rounded = (resid_grad * slope[rows, :]).astype(bf16).astype(f32)
        put_shifted(cab, last, row, rounded)
        vgrad[2:3, :] += jnp.sum(rounded, axis=0, keepdims=True)
        return 0

    def idle_step(i, _):
        rows = pl.ds(mult(i * ROWS, ROWS), ROWS)
        resid_out[rows, :] = grad[rows, :].astype(f32)
        return 0

    lax.fori_loop(0, blocks, row_step, 0)
    lax.fori_loop(blocks, seq // ROWS, idle_step, 0)

    end_shifted(cab, last, length, blocks, seq // ROWS)


def ffn_weight_grad(place, sec, hg, mg, act, keep, give, hbgrad):
    seq, full = sec.shape
    di, part = keep.shape[4:]
    sec_t = jnp.concatenate([sec[...].T, jnp.ones((16, seq), bf16)])
    mg_t = mg[...].T
    for half, ref in enumerate((keep, give)):
        parity = (place[1] & 1) ^ half
        for j in range(keep.shape[1]):
            cols = pl.ds(mult((parity + 2 * j) * part, part), part)
            for w, (left, right) in enumerate(((sec_t, hg), (mg_t, act))):
                value = dot(left, right[:, cols])
                if w == 0:
                    hbgrad[0:1, cols] = value[full : full + 1, :]
                value = value.astype(bf16)
                for d in range(full // di):
                    index = share_index(place, d, parity, j)
                    ref[(*index, w)] = value[d * di : (d + 1) * di, :]


def shifted_rows(cab, u, row, count):
    odd = u & 1
    return cab[odd, pl.ds(mult(row + (u - odd) * DILATION, 16), count), :]


def conv_weight_grad(place, na, cab, keep, *gives):
    seq, full = na.shape
    taps, di, own = keep.shape[3:]
    na_t = na[...].T
    for t in range(taps):
        u = KERNEL - 1 - t
        odd = u & 1
        rows = pl.ds((u - odd) * DILATION, seq)
        group, local = divmod(t, gives[0].shape[3])
        for half, (ref, tap) in enumerate(((keep, t), (gives[group], local))):
            parity = (place[1] & 1) ^ half
            blocks = range(keep.shape[1])
            cols = [pl.ds(mult((parity + 2 * j) * own, own), own) for j in blocks]
            right = jnp.concatenate([cab[odd, rows, c] for c in cols], axis=1)
            value = dot(na_t, right).astype(bf16)
            for j in blocks:
                for d in range(full // di):
                    index = share_index(place, d, parity, j)
                    ref[(*index, tap)] = value[d * di : (d + 1) * di, j * own : (j + 1) * own]


def pair_sum(place, keep, r0, r1, r2, onward, own):
    count = r0.shape[3]
    for group, received in enumerate((r0, r1, r2)):
        taps = pl.ds(group * count, count)
        for a in range(keep.shape[1]):
            both = keep[1, a, :, taps].astype(f32) + received[1, a].astype(f32)
            onward[a, :, taps] = both.astype(bf16)
            own[a, :, taps] = keep[0, a, :, taps].astype(f32) + received[0, a].astype(f32)


def conv_backward(place, x_full, cab, resid, w, vec, *rest):
    outs, (vgrad, values_ref) = rest[:4], rest[4:]
    seq, full = x_full.shape
    blocks = place[3]
    vgrad[...] = jnp.zeros_like(vgrad)

    def in_store(rows, values):
        values_ref[...] = values.astype(bf16)
        store_columns(place, outs, rows, values_ref)

    def row_step(i, _):
        row = mult(i * ROWS, ROWS)
        rows = pl.ds(row, ROWS)
        total = jnp.zeros((ROWS, full), f32)
        for t in range(KERNEL):
            shifted = shifted_rows(cab, KERNEL - 1 - t, row, ROWS)
            total = total + dot(shifted, w[t], NT)
        s, inverse = norm_parts(x_full[rows, :].astype(f32))
        vgrad[0:1, :] += jnp.sum(total * s, axis=0, keepdims=True)
        vgrad[1:2, :] += jnp.sum(total, axis=0, keepdims=True)
        in_store(rows, resid[rows, :] + norm_back(total * vec[0:1, :], s, inverse))
        return 0

    def idle_step(i, _):
        rows = pl.ds(mult(i * ROWS, ROWS), ROWS)
        in_store(rows, resid[rows, :])
        return 0

    lax.fori_loop(0, blocks, row_step, 0)
    lax.fori_loop(blocks, seq // ROWS, idle_step, 0)


def tie(*values):
    return lax.optimization_barrier(values)


def placed(kernel):
    def run(lengths, *refs):
        mp = lax.axis_index("mp")
        length = lengths[mp]
        kernel((lax.axis_index("dp"), mp, length, length // ROWS), *refs)

    return run


def call(kernel, lengths, args, outs, scratch, flops, mib, far=(), far_out=()):
    near = pl.BlockSpec(memory_space=pltpu.VMEM)
    left = pl.BlockSpec(memory_space=pltpu.HBM)
    moved = sum(a.size * a.dtype.itemsize for a in (*args, *outs))
    return pl.pallas_call(
        placed(kernel),
        out_shape=outs,
        in_specs=[pl.BlockSpec(memory_space=pltpu.SMEM)]
        + [left if i in far else near for i in range(len(args))],
        out_specs=[left if i in far_out else near for i in range(len(outs))],
        scratch_shapes=scratch,
        compiler_params=pltpu.CompilerParams(vmem_limit_bytes=mib * 2**20),
        cost_estimate=pl.CostEstimate(flops=flops, bytes_accessed=moved, transcendentals=0),
    )(lengths, *args)


def total_share(place, conv_own, c1, c2, c3, ffn_share, v1, v2, bias_grad, conv_share, small):
    full = small.shape[1]
    total = conv_own[...]
    for part in (c1, c2, c3):
        total = total + part[...].astype(f32)
    conv_share[...] = total
    squares = jnp.sum(total * total) + jnp.sum(ffn_share[...] * ffn_share[...])
    small[0:6, :] = (v1[...] + v2[...])[0:6, :]
    units = bias_grad.shape[1] // full
    for row in range(units):
        small[6 + row : 7 + row, :] = bias_grad[:, row * full : (row + 1) * full]
    small[6 + units :, :] = jnp.full((small.shape[0] - 6 - units, full), squares, f32)


def adam(weight, first_mom, second, gradient, clip_scale, step_rate, decay_rate):
    clipped = gradient * clip_scale
    first_new = BETA_ONE * first_mom + (1.0 - BETA_ONE) * clipped
    second_new = BETA_TWO * second + (1.0 - BETA_TWO) * clipped * clipped
    update_dir = (
        first_new
        / (1.0 - BETA_ONE**STEP)
        / (jnp.sqrt(second_new / (1.0 - BETA_TWO**STEP)) + ADAM_EPS)
    )
    return (weight - step_rate * (update_dir + decay_rate * weight), first_new, second_new)


def update(place, small, small_far, conv_share, ffn_share, *rest):
    states, outs, total = rest[:15], rest[15:31], rest[31]
    total[...] = small[...] + small_far[...]
    rows = total.shape[0] - 1
    own_rows = total[0:rows, :]
    squares = jnp.sum(own_rows * own_rows, axis=(0, 1), keepdims=True) + total[rows:, 0:1]
    norm = jnp.sqrt(squares)
    outs[15][...] = jnp.broadcast_to(norm, outs[15].shape)
    clip_scale = jnp.minimum(1.0, CLIP_NORM / (norm + 1e-06))
    gradients = [
        conv_share[...],
        ffn_share[0],
        ffn_share[1],
        total[0:6, :],
        total[pl.ds(6 + place[1], 1), :],
    ]
    for i, gradient in enumerate(gradients):
        rates = (MATRIX_RATE, WEIGHT_DECAY) if i < 3 else (VECTOR_RATE, 0.0)
        scale = clip_scale.reshape((1,) * gradient.ndim)
        state = [ref[...] for ref in states[3 * i : 3 * i + 3]]
        for ref, value in zip(outs[3 * i : 3 * i + 3], adam(*state, gradient, scale, *rates)):
            ref[...] = value


def per_device(
    ndp,
    nmp,
    inputs,
    cotangent,
    lengths,
    conv_master,
    hidden_master,
    output_master,
    conv_first,
    hidden_first,
    output_first,
    conv_second,
    hidden_second,
    output_second,
    vectors,
    vector_first,
    vector_second,
    hidden_bias,
    bias_first,
    bias_second,
):
    axes = ("dp", "mp")
    nz = ndp // 2
    seq, own = inputs.shape[1:]
    full = vectors.shape[1]
    part = hidden_bias.shape[0]
    hidden = part * nmp
    di = full // ndp
    mp = lax.axis_index("mp")

    def perm(move):
        pairs = []
        for i in range(ndp * nmp):
            d, m = divmod(i, nmp)
            z, x, y, c = move(d >> 1, d & 1, m >> 1, m & 1)
            pairs.append((i, (z * 2 + x) * nmp + y * 2 + c))
        return pairs

    across_z = [perm(lambda z, x, y, c, k=k: (z ^ k, x, y, c)) for k in range(nz)]
    step_x = perm(lambda z, x, y, c: (z, x ^ 1, y, c))
    step_y = perm(lambda z, x, y, c: (z, x, y ^ 1, c))
    step_c = perm(lambda z, x, y, c: (z, x, y, c ^ 1))
    step_xy = perm(lambda z, x, y, c: (z, x ^ 1, y, c) if c == 0 else (z, x, y ^ 1, c))
    step_yx = perm(lambda z, x, y, c: (z, x, y ^ 1, c) if c == 0 else (z, x ^ 1, y, c))
    within = [[(i, i ^ k) for i in range(nmp)] for k in range(nmp)]

    def send(values, pairs):
        return lax.ppermute(values, axes, pairs)

    def gather_z(shard):
        return [shard] + [send(shard, across_z[k]) for k in range(1, nz)]

    def add(*terms):
        total = terms[0].astype(f32)
        for term in terms[1:]:
            total = total + term.astype(f32)
        return total

    def scatter_b(k, r):
        return add(k[1], r[1]).astype(bf16)

    def scatter_a(k, r, rb):
        return add(k[0, 1], r[0, 1], rb[1]).astype(bf16)

    def scatter_z(*terms):
        own_part = add(*(t[0] for t in terms))
        parts = [add(*(t[j] for t in terms)).astype(bf16) for j in range(1, nz)]
        return own_part, [send(part_of, across_z[j + 1]) for j, part_of in enumerate(parts)]

    def take_windows(values, extra=None):
        blocks = [lax.dynamic_index_in_dim(values, mp ^ k, 0, False) for k in range(nmp)]
        if extra is not None:
            blocks = [jnp.concatenate([block, extra]) for block in blocks]
        return blocks

    def swap(blocks):
        return [blocks[0]] + [lax.ppermute(blocks[k], "mp", within[k]) for k in range(1, nmp)]

    def in_order(pieces):
        for bit in range(nmp.bit_length() - 1):
            odd = ((mp >> bit) & 1) == 1
            pieces = [jnp.where(odd, pieces[k ^ (1 << bit)], pieces[k]) for k in range(nmp)]
        return jnp.stack(pieces)

    def all_sum(values):
        values = values + send(values, step_c)
        step = 1
        while step < nz:
            values = values + send(values, across_z[step])
            step *= 2
        values = values + send(values, step_x)
        return values, send(values, step_y)

    exact, rest = [], hidden_bias
    for _ in range(3):
        exact.append(lax.reduce_precision(rest, 8, 7))
        rest = rest - exact[-1]
    exact.append(jnp.zeros_like(rest))
    exact = jnp.concatenate(exact).reshape(4 * part // own, own).astype(bf16)
    ffn_shard = jnp.stack([hidden_master.astype(bf16), output_master.astype(bf16).T])

    x_blocks = take_windows(inputs, exact)
    *x_blocks, conv_shard = tie(*x_blocks, conv_master.astype(bf16))
    x_parts = swap(x_blocks)
    conv_z = gather_z(conv_shard)
    ffn_y = send(ffn_shard, step_y)
    *tied, ffn_shard, ffn_y = tie(*x_parts, *conv_z, ffn_shard, ffn_y)
    x_parts, conv_z = tied[:nmp], jnp.stack(tied[nmp:])
    first, last = [jnp.stack([ffn_shard[w], ffn_y[w]]) for w in (0, 1)]
    conv_a, conv_b = send(conv_z, step_xy), send(conv_z, step_yx)
    first = gather_z(first)
    conv_z, conv_a, conv_b, last, *first = tie(conv_z, conv_a, conv_b, last, *first)
    conv_ab = send(conv_a, step_yx)
    first = jnp.stack(first)
    first_x = send(first, step_x)
    last = gather_z(last)
    conv_z, conv_a, conv_b, conv_ab, cotangent, first, first_x, *last = tie(
        conv_z, conv_a, conv_b, conv_ab, cotangent, first, first_x, *last
    )
    conv_parts = [conv_z, conv_a, conv_b, conv_ab]
    conv_parts += [send(part_of, step_c) for part_of in conv_parts]
    last = jnp.stack(last)
    last_x = send(last, step_x)
    c_blocks = take_windows(cotangent)
    c_parts = [lax.ppermute(c_blocks[k], "mp", within[k]) for k in range(2, nmp)]

    S = jax.ShapeDtypeStruct
    padded = seq + 2 * REACH
    last, *x_parts = tie(last, *x_parts)
    first_c, last_c = send(first, step_c), send(last, step_c)
    w_full, x_full, normed, residual, slope, bias_all = call(
        conv_forward,
        lengths,
        (*x_parts, vectors, *conv_parts),
        (
            S((KERNEL, full, full), bf16),
            S((seq, full), bf16),
            S((seq, full), bf16),
            *(S((seq, full), f32),) * 2,
            S((nmp, part // own, own), f32),
        ),
        [
            pltpu.VMEM((2, padded, full), bf16),
            pltpu.VMEM((DILATION, full), f32),
            pltpu.VMEM((KERNEL, full, full), bf16),
            pltpu.VMEM((nmp, 4 * part // own, own), bf16),
            pltpu.SemaphoreType.DMA((8, nz)),
            pltpu.SemaphoreType.DMA((3, nmp)),
        ],
        2 * seq * KERNEL * full * full,
        24,
        (0, 1, 2, 3, *range(5, 13)),
        (0,),
    )
    *tied, residual = tie(first, first_x, first_c, last, last_x, last_c, *c_blocks[:2], *c_parts, residual)
    first, first_x, first_c, last, last_x, last_c, *c_parts = tied
    c_parts[1] = lax.ppermute(c_parts[1], "mp", within[1])
    ffn_parts = [first, first_x, first_c, send(first_x, step_c)]
    ffn_parts += [last, last_x, last_c, send(last_x, step_c)]
    *block_parts, active, hidden_grad, second, mix_grad, hidden_full = call(
        ffn_hidden,
        lengths,
        (x_full, residual, *c_parts, vectors, bias_all.reshape(1, hidden), *ffn_parts),
        (
            *(S((seq, own), bf16),) * nmp,
            *(S((seq, hidden), bf16),) * 2,
            *(S((seq, full), bf16),) * 2,
            S((full, hidden), bf16),
        ),
        [
            pltpu.VMEM((2, full, hidden), bf16),
            pltpu.VMEM((ROWS, full), bf16),
            pltpu.SemaphoreType.DMA((8, nz, 2)),
            pltpu.SemaphoreType.DMA((2, nmp)),
        ],
        6 * seq * hidden * full,
        20,
        (2, 3, 4, 5, *range(8, 16)),
        (8,),
    )
    for k in (1, 2):
        block_parts[k] = lax.ppermute(block_parts[k], "mp", within[k])
    ffn_keep, ffn_give, bias_grad = call(
        ffn_weight_grad,
        lengths,
        (second, hidden_grad, mix_grad, active),
        (*(S((2, 2, nz, 2, di, part), bf16),) * 2, S((1, hidden), f32)),
        [],
        1,
        12,
    )
    ffn_give, ffn_keep, hidden_grad, *block_parts[1:] = tie(
        ffn_give, ffn_keep, hidden_grad, *block_parts[1:]
    )
    ffn_r = send(ffn_give, step_c)
    block_parts[3] = lax.ppermute(block_parts[3], "mp", within[3])
    resid_grad, conv_grad, vgrad_two = call(
        norm_backward,
        lengths,
        (residual, slope, mix_grad, hidden_grad, hidden_full, vectors),
        (S((seq, full), f32), S((2, padded, full), bf16), S((8, full), f32)),
        [pltpu.VMEM((DILATION, full), f32)],
        1,
        16,
    )
    ffn_sum, conv_grad, block_parts[3] = tie(scatter_b(ffn_keep, ffn_r), conv_grad, block_parts[3])
    ffn_rb = send(ffn_sum, step_yx)
    conv_keep, *conv_give = call(
        conv_weight_grad,
        lengths,
        (normed, conv_grad),
        (S((2, 2, nz, KERNEL, di, own), bf16), *(S((2, 2, nz, KERNEL // 3, di, own), bf16),) * 3),
        [],
        1,
        16,
    )
    *conv_give, conv_keep, conv_grad = tie(*conv_give, conv_keep, conv_grad)
    conv_r = [send(give, step_c) for give in conv_give]
    *in_parts, vgrad_one = call(
        conv_backward,
        lengths,
        (x_full, conv_grad, resid_grad, w_full, vectors),
        (*(S((seq, own), bf16),) * nmp, S((8, full), f32)),
        [pltpu.VMEM((ROWS, full), bf16)],
        1,
        16,
    )
    ffn_sum = scatter_a(ffn_keep, ffn_r, ffn_rb)
    *conv_r, ffn_sum, in_parts[1] = tie(*conv_r, ffn_sum, in_parts[1])
    conv_sum, conv_own = call(
        pair_sum,
        lengths,
        (conv_keep, *conv_r),
        (S((2, nz, KERNEL, di, own), bf16), S((2, nz, KERNEL, di, own), f32)),
        [],
        1,
        16,
    )
    conv_rb = send(conv_sum, step_yx)
    ffn_ra = send(ffn_sum, step_xy)
    ffn_own, ffn_rest = scatter_z(ffn_keep[0, 0], ffn_r[0, 0], ffn_rb[0], ffn_ra)
    ffn_share = add(ffn_own, *ffn_rest)
    conv_ra = send(add(conv_own[1], conv_rb[1]).astype(bf16), step_xy)
    conv_ra, *in_parts[2:] = tie(conv_ra, *in_parts[2:])
    conv_own, conv_rest = scatter_z(conv_own[0], conv_rb[0], conv_ra)
    for part_of in conv_rest[3:]:
        conv_own = conv_own + part_of.astype(f32)
    for k in range(1, nmp):
        in_parts[k] = lax.ppermute(in_parts[k], "mp", within[k])
    conv_own, *tied = tie(conv_own, *conv_rest[:3], *in_parts)
    conv_rest, in_parts = tied[:3], tied[3:]
    block_output = in_order(block_parts)
    input_grad = in_order(in_parts).astype(f32)

    conv_share, small = call(
        total_share,
        lengths,
        (conv_own, *conv_rest, ffn_share, vgrad_one, vgrad_two, bias_grad),
        (S((KERNEL, di, own), f32), S((7 + hidden // full, full), f32)),
        [],
        1,
        16,
    )
    small, small_far = all_sum(small)
    matrices = (
        *(conv_master, conv_first, conv_second),
        *(hidden_master, hidden_first, hidden_second),
        *(output_master.T, output_first.T, output_second.T),
    )
    vector_ones = (vectors, vector_first, vector_second)
    bias_ones = [v.reshape(1, part) for v in (hidden_bias, bias_first, bias_second)]
    states = (*matrices, *vector_ones, *bias_ones)
    *updated, norm = call(
        update,
        lengths,
        (small, small_far, conv_share, ffn_share, *states),
        (*(S(v.shape, f32) for v in states), S((1, 1), f32)),
        [pltpu.VMEM(small.shape, f32)],
        1,
        16,
    )
    updated[6:9] = [v.T for v in updated[6:9]]
    updated[12:] = [v.reshape(part) for v in updated[12:]]
    return (block_output, input_grad, norm.reshape(()), *updated)


def solution(mesh):
    rows = P("dp", None, "mp")
    conv = P(None, "dp", "mp")
    hid = P("dp", "mp")
    out = P("mp", "dp")
    return jax.shard_map(
        functools.partial(per_device, mesh.shape["dp"], mesh.shape["mp"]),
        mesh=mesh,
        in_specs=(rows, rows, P("dp"), *(conv, hid, out) * 3, *(P(),) * 3, *(P("mp"),) * 3),
        out_specs=(
            rows,
            rows,
            P(),
            *(conv,) * 3,
            *(hid,) * 3,
            *(out,) * 3,
            *(P(),) * 3,
            *(P("mp"),) * 3,
        ),
        check_vma=False,
    )
```

profile of v0, /device:TPU:0, one launch (start us, length us, event | category | flops | bytes accessed | tf_op | source)
XLA Modules:
  0.0 197.1 jit_solution(3863059861638260571)
XLA Ops:
  3.4 3.1 %collective-permute-start.3 = (bf16[9,64,128]{2,1,0:T(8,128)(2,1)S(1)}, bf16[9,64,128]{2,1,0:T(8,128)(2,1)S(1)}, u32[]{:S(2)}, u32[]{:S(2)}) collective-permute-start(bf16[9,64,128]{2,1,0:T(8,128)(2,1)S(1)} %convert_element_type.201), channel_id=1, source_target_pairs={{0,8},{1,9},{2,10},{3,11},{4,12},{5,13},{6,14},{7,15},{8,0},{9,1},... | collective-permute-start | bytes 442376 | tf_op jit(solution)/shard_map/ppermute | solution.py:522
  10.0 2.0 %collective-permute-done.6 = bf16[2,64,512]{2,1,0:T(8,128)(2,1)S(1)} collective-permute-done((bf16[2,64,512]{2,1,0:T(8,128)(2,1)S(1)}, bf16[2,64,512]{2,1,0:T(8,128)(2,1)S(1)}, u32[]{:S(2)}, u32[]{:S(2)}) %collective-permute-start.6) | collective-permute-done | bytes 131104 | tf_op jit(solution)/shard_map/ppermute | solution.py:522
  12.0 2.6 %collective-permute-start.4 = (bf16[9,64,128]{2,1,0:T(8,128)(2,1)S(1)}, bf16[9,64,128]{2,1,0:T(8,128)(2,1)S(1)}, u32[]{:S(2)}, u32[]{:S(2)}) collective-permute-start(bf16[9,64,128]{2,1,0:T(8,128)(2,1)S(1)} %convert_element_type.201), channel_id=1, source_target_pairs={{0,16},{1,17},{2,18},{3,19},{4,20},{5,21},{6,22},{7,23},{8,24},{9,... | collective-permute-start | bytes 442376 | tf_op jit(solution)/shard_map/ppermute | solution.py:522
  14.9 9.5 %collective-permute-done.4 = bf16[9,64,128]{2,1,0:T(8,128)(2,1)S(1)} collective-permute-done((bf16[9,64,128]{2,1,0:T(8,128)(2,1)S(1)}, bf16[9,64,128]{2,1,0:T(8,128)(2,1)S(1)}, u32[]{:S(2)}, u32[]{:S(2)}) %collective-permute-start.4) | collective-permute-done | bytes 147488 | tf_op jit(solution)/shard_map/ppermute | solution.py:522
  28.0 3.3 %collective-permute-start.10 = (bf16[2,64,512]{2,1,0:T(8,128)(2,1)S(1)}, bf16[2,64,512]{2,1,0:T(8,128)(2,1)S(1)}, u32[]{:S(2)}, u32[]{:S(2)}) collective-permute-start(bf16[2,64,512]{2,1,0:T(8,128)(2,1)S(1)} %pad_maximum_fusion.6), channel_id=1, source_target_pairs={{0,16},{1,17},{2,18},{3,19},{4,20},{5,21},{6,22},{7,23},{8,24},{9,... | collective-permute-start | bytes 393224 | tf_op jit(solution)/shard_map/ppermute | solution.py:522
  32.5 7.4 %collective-permute-done.10 = bf16[2,64,512]{2,1,0:T(8,128)(2,1)S(1)} collective-permute-done((bf16[2,64,512]{2,1,0:T(8,128)(2,1)S(1)}, bf16[2,64,512]{2,1,0:T(8,128)(2,1)S(1)}, u32[]{:S(2)}, u32[]{:S(2)}) %collective-permute-start.10) | collective-permute-done | bytes 131104 | tf_op jit(solution)/shard_map/ppermute | solution.py:522
  41.9 2.6 %collective-permute-start.14 = (bf16[2,64,512]{2,1,0:T(8,128)(2,1)S(1)}, bf16[2,64,512]{2,1,0:T(8,128)(2,1)S(1)}, u32[]{:S(2)}, u32[]{:S(2)}) collective-permute-start(bf16[2,64,512]{2,1,0:T(8,128)(2,1)S(1)} %pad_maximum_fusion.5), channel_id=1, source_target_pairs={{0,8},{1,9},{2,10},{3,11},{4,12},{5,13},{6,14},{7,15},{8,0},{9,1},... | collective-permute-start | bytes 393224 | tf_op jit(solution)/shard_map/ppermute | solution.py:522
  48.9 7.5 %collective-permute-done.15 = bf16[2,64,512]{2,1,0:T(8,128)(2,1)S(1)} collective-permute-done((bf16[2,64,512]{2,1,0:T(8,128)(2,1)S(1)}, bf16[2,64,512]{2,1,0:T(8,128)(2,1)S(1)}, u32[]{:S(2)}, u32[]{:S(2)}) %collective-permute-start.15) | collective-permute-done | bytes 131104 | tf_op jit(solution)/shard_map/ppermute | solution.py:522
  56.4 2.4 %collective-permute-start.17 = (bf16[4,9,64,128]{3,2,1,0:T(8,128)(2,1)S(1)}, bf16[4,9,64,128]{3,2,1,0:T(8,128)(2,1)S(1)}, u32[]{:S(2)}, u32[]{:S(2)}) collective-permute-start(bf16[4,9,64,128]{3,2,1,0:T(8,128)(2,1)S(1)} %pad_maximum_fusion.1.refs_5_), channel_id=1, source_target_pairs={{0,1},{1,0},{2,3},{3,2},{4,5},{5,4},{6,7},{7,6},{8,9},{9,8},{10,11... | collective-permute-start | bytes 1769480 | tf_op jit(solution)/shard_map/ppermute | solution.py:522
  63.8 4.5 %shard_map.313 = (bf16[9,512,512]{2,1,0:T(8,128)(2,1)S(1)}, bf16[1024,512]{1,0:T(8,128)(2,1)S(1)}, bf16[1024,512]{1,0:T(8,128)(2,1)S(1)}, f32[1024,512]{1,0:T(8,...) custom-call(s32[4]{0:T(128)S(1)} %copy-done.10, bf16[1040,128]{1,0:T(8,128)(2,1)S(1)} %concatenate.28.refs_0_, ...), custom_call_target="tpu_custom_call" | custom-call | flops 4831838208 | bytes 16814080 | tf_op jit(solution)/shard_map/pallas_call | solution.py:412
  68.3 2.9 %collective-permute-done.24.refs_4_ = bf16[1024,128]{1,0:T(8,128)(2,1)S(1)} collective-permute-done((bf16[1024,128]{1,0:T(8,128)(2,1)S(1)}, bf16[1024,128]{1,0:T(8,128)(2,1)S(1)}, u32[]{:S(2)}, u32[]{:S(2)}) %collective-permute-start.24) | collective-permute-done | bytes 262176 | tf_op jit(solution)/shard_map/ppermute | solution.py:599
  71.2 4.5 %collective-permute-done.25.refs_5_ = bf16[1024,128]{1,0:T(8,128)(2,1)S(1)} collective-permute-done((bf16[1024,128]{1,0:T(8,128)(2,1)S(1)}, bf16[1024,128]{1,0:T(8,128)(2,1)S(1)}, u32[]{:S(2)}, u32[]{:S(2)}) %collective-permute-start.25) | collective-permute-done | bytes 262176 | tf_op jit(solution)/shard_map/ppermute | solution.py:599
  76.7 2.2 %collective-permute-done.26.refs_3_ = bf16[1024,128]{1,0:T(8,128)(2,1)S(1)} collective-permute-done((bf16[1024,128]{1,0:T(8,128)(2,1)S(1)}, bf16[1024,128]{1,0:T(8,128)(2,1)S(1)}, u32[]{:S(2)}, u32[]{:S(2)}) %collective-permute-start.26) | collective-permute-done | bytes 262176 | tf_op jit(solution)/shard_map/ppermute | solution.py:631
  78.8 6.0 %shard_map.314 = (bf16[1024,128]{1,0:T(8,128)(2,1)S(1)}, bf16[1024,128]{1,0:T(8,128)(2,1)S(1)}, bf16[1024,128]{1,0:T(8,128)(2,1)S(1)}, bf16[1024,128]{1,0:T(8,12...) custom-call(s32[4]{0:T(128)S(1)} %copy-done.10, ...), custom_call_target="tpu_custom_call" | custom-call | flops 6442450944 | bytes 22040576 | tf_op jit(solution)/shard_map/pallas_call | solution.py:412
  85.3 2.7 %collective-permute-start.30 = (bf16[1024,128]{1,0:T(8,128)(2,1)S(1)}, bf16[1024,128]{1,0:T(8,128)(2,1)S(1)}, u32[]{:S(2)}, u32[]{:S(2)}) collective-permute-start(bf16[1024,128]{1,0:T(8,128)(2,1)S(1)} %get-tuple-element.208), channel_id=1, source_target_pairs={{0,2},{1,3},{2,0},{3,1},{4,6},{5,7},{6,4},{7,5},{8,10},{9,11},{10,... | collective-permute-start | bytes 786440 | tf_op jit(solution)/shard_map/ppermute | solution.py:656
  87.9 5.2 %shard_map.315 = (bf16[2,2,4,2,64,512]{5,4,3,2,1,0:T(8,128)(2,1)S(1)}, bf16[2,2,4,2,64,512]{5,4,3,2,1,0:T(8,128)(2,1)S(1)}, f32[1,2048]{1,0:T(1,128)S(1)}) custom-call(s32[4]{0:T(128)S(1)} %copy-done.10, bf16[1024,512]{1,0:T(8,128)(2,1)S(1)} %get-tuple-element.201.refs_0_, bf16[1024,2048]{1,0:T(8,128)(2,1)S(1)} %get-tuple-element.213.refs_1_.refs_3_, ...), custom_call_target="tpu_custom_call" | custom-call | flops 1 | bytes 14688256 | tf_op jit(solution)/shard_map/pallas_call | solution.py:412
  99.0 3.7 %collective-permute-done.32 = bf16[1024,128]{1,0:T(8,128)(2,1)S(1)} collective-permute-done((bf16[1024,128]{1,0:T(8,128)(2,1)S(1)}, bf16[1024,128]{1,0:T(8,128)(2,1)S(1)}, u32[]{:S(2)}, u32[]{:S(2)}) %collective-permute-start.32) | collective-permute-done | bytes 262176 | tf_op jit(solution)/shard_map/ppermute | solution.py:670
  104.2 5.9 %shard_map.317 = (bf16[2,2,4,9,64,128]{5,4,3,2,1,0:T(8,128)(2,1)S(1)}, bf16[2,2,4,3,64,128]{5,4,3,2,1,0:T(8,128)(2,1)S(1)}, bf16[2,2,4,3,64,128]{5,4,3,2,1,0:T(8...) custom-call(s32[4]{0:T(128)S(1)} %copy-done.10, bf16[1024,512]{1,0:T(8,128)(2,1)S(1)} %get-tuple-element.221.refs_0_, ...), custom_call_target="tpu_custom_call" | custom-call | flops 1 | bytes 7995392 | tf_op jit(solution)/shard_map/pallas_call | solution.py:412
  112.2 2.7 %shard_map.318 = (bf16[1024,128]{1,0:T(8,128)(2,1)S(1)}, bf16[1024,128]{1,0:T(8,128)(2,1)S(1)}, bf16[1024,128]{1,0:T(8,128)(2,1)S(1)}, bf16[1024,128]{1,0:T(8,128)(2,1)S(1)}, f32[8,512]{1,0:T(8,128)S(1)}) custom-call(s32[4]{0:T(128)S(1)} %copy-done.10, bf16[1024,512]{1,0:T(8,128)(2,1)S(1)} %get-tuple-element.183.refs_0_, ...), custom_call_target="tpu_custom_call" | custom-call | flops 1 | bytes 11169792 | tf_op jit(solution)/shard_map/pallas_call | solution.py:412
  114.8 2.6 %collective-permute-done.36 = bf16[2,4,2,64,512]{4,3,2,1,0:T(8,128)(2,1)S(1)} collective-permute-done((bf16[2,4,2,64,512]{4,3,2,1,0:T(8,128)(2,1)S(1)}, bf16[2,4,2,64,512]{4,3,2,1,0:T(8,128)(2,1)S(1)}, u32[]{:S(2)}, u32[]{:S(2)}) %collective-permute-start.36) | collective-permute-done | bytes 1048608 | tf_op jit(solution)/shard_map/ppermute | solution.py:522
  122.2 18.5 %collective-permute-done.37 = bf16[2,4,9,64,128]{4,3,2,1,0:T(8,128)(2,1)S(1)} collective-permute-done((bf16[2,4,9,64,128]{4,3,2,1,0:T(8,128)(2,1)S(1)}, bf16[2,4,9,64,128]{4,3,2,1,0:T(8,128)(2,1)S(1)}, u32[]{:S(2)}, u32[]{:S(2)}) %collective-permute-start.37) | collective-permute-done | bytes 1179680 | tf_op jit(solution)/shard_map/ppermute | solution.py:522
  142.7 6.7 %collective-permute-start.46 = (bf16[2,64,512]{2,1,0:T(8,128)(2,1)S(1)}, bf16[2,64,512]{2,1,0:T(8,128)(2,1)S(1)}, u32[]{:S(2)}, u32[]{:S(2)}) collective-permute-start(bf16[2,64,512]{2,1,0:T(8,128)(2,1)S(1)} %get-tuple-element.278), channel_id=1, source_target_pairs={{0,8},{1,9},{2,10},{3,11},{4,12},{5,13},{6,14},{7,15},{8,0},{9,1},... | collective-permute-start | bytes 393224 | tf_op jit(solution)/shard_map/ppermute | solution.py:522
  149.3 2.4 %collective-permute-start.47 = (bf16[2,64,512]{2,1,0:T(8,128)(2,1)S(1)}, bf16[2,64,512]{2,1,0:T(8,128)(2,1)S(1)}, u32[]{:S(2)}, u32[]{:S(2)}) collective-permute-start(bf16[2,64,512]{2,1,0:T(8,128)(2,1)S(1)} %get-tuple-element.280), channel_id=1, source_target_pairs={{0,16},{1,17},{2,18},{3,19},{4,20},{5,21},{6,22},{7,23},{8,24},{9,... | collective-permute-start | bytes 393224 | tf_op jit(solution)/shard_map/ppermute | solution.py:522
  153.4 2.0 %collective-permute-done.46 = bf16[2,64,512]{2,1,0:T(8,128)(2,1)S(1)} collective-permute-done((bf16[2,64,512]{2,1,0:T(8,128)(2,1)S(1)}, bf16[2,64,512]{2,1,0:T(8,128)(2,1)S(1)}, u32[]{:S(2)}, u32[]{:S(2)}) %collective-permute-start.46) | collective-permute-done | bytes 131104 | tf_op jit(solution)/shard_map/ppermute | solution.py:522
  155.3 2.4 %collective-permute-start.39 = (bf16[9,64,128]{2,1,0:T(8,128)(2,1)S(1)}, bf16[9,64,128]{2,1,0:T(8,128)(2,1)S(1)}, u32[]{:S(2)}, u32[]{:S(2)}) collective-permute-start(bf16[9,64,128]{2,1,0:T(8,128)(2,1)S(1)} %get-tuple-element.283), channel_id=1, source_target_pairs={{0,8},{1,9},{2,10},{3,11},{4,12},{5,13},{6,14},{7,15},{8,0},{9,1},... | collective-permute-start | bytes 442376 | tf_op jit(solution)/shard_map/ppermute | solution.py:522
  157.8 4.5 %collective-permute-done.47 = bf16[2,64,512]{2,1,0:T(8,128)(2,1)S(1)} collective-permute-done((bf16[2,64,512]{2,1,0:T(8,128)(2,1)S(1)}, bf16[2,64,512]{2,1,0:T(8,128)(2,1)S(1)}, u32[]{:S(2)}, u32[]{:S(2)}) %collective-permute-start.47) | collective-permute-done | bytes 131104 | tf_op jit(solution)/shard_map/ppermute | solution.py:522
  162.3 2.8 %collective-permute-start.41 = (bf16[9,64,128]{2,1,0:T(8,128)(2,1)S(1)}, bf16[9,64,128]{2,1,0:T(8,128)(2,1)S(1)}, u32[]{:S(2)}, u32[]{:S(2)}) collective-permute-start(bf16[9,64,128]{2,1,0:T(8,128)(2,1)S(1)} %get-tuple-element.281), channel_id=1, source_target_pairs={{0,24},{1,25},{2,26},{3,27},{4,28},{5,29},{6,30},{7,31},{8,16},{9,... | collective-permute-start | bytes 442376 | tf_op jit(solution)/shard_map/ppermute | solution.py:522
  166.3 9.4 %collective-permute-done.40.refs_2_ = bf16[9,64,128]{2,1,0:T(8,128)(2,1)S(1)} collective-permute-done((bf16[9,64,128]{2,1,0:T(8,128)(2,1)S(1)}, bf16[9,64,128]{2,1,0:T(8,128)(2,1)S(1)}, u32[]{:S(2)}, u32[]{:S(2)}) %collective-permute-start.40) | collective-permute-done | bytes 147488 | tf_op jit(solution)/shard_map/ppermute | solution.py:522
  177.8 2.1 %collective-permute-start.50 = (f32[11,512]{1,0:T(8,128)S(1)}, f32[11,512]{1,0:T(8,128)S(1)}, u32[]{:S(2)}, u32[]{:S(2)}) collective-permute-start(f32[11,512]{1,0:T(8,128)S(1)} %add.179), channel_id=1, source_target_pairs={{0,8},{1,9},{2,10},{3,11},{4,12},{5,13},{6,14},{7,15},{8,0},{9,1},... | collective-permute-start | bytes 67592 | tf_op jit(solution)/shard_map/ppermute | solution.py:522
  181.8 2.6 %collective-permute-start.51 = (f32[11,512]{1,0:T(8,128)S(1)}, f32[11,512]{1,0:T(8,128)S(1)}, u32[]{:S(2)}, u32[]{:S(2)}) collective-permute-start(f32[11,512]{1,0:T(8,128)S(1)} %add.180), channel_id=1, source_target_pairs={{0,16},{1,17},{2,18},{3,19},{4,20},{5,21},{6,22},{7,23},{8,24},{9,... | collective-permute-start | bytes 67592 | tf_op jit(solution)/shard_map/ppermute | solution.py:522
  187.7 2.8 %collective-permute-done.52 = f32[11,512]{1,0:T(8,128)S(1)} collective-permute-done((f32[11,512]{1,0:T(8,128)S(1)}, f32[11,512]{1,0:T(8,128)S(1)}, u32[]{:S(2)}, u32[]{:S(2)}) %collective-permute-start.52) | collective-permute-done | bytes 22560 | tf_op jit(solution)/shard_map/ppermute | solution.py:522
  194.6 2.3 %shard_map.321 = (f32[9,64,128]{2,1,0:T(8,128)}, f32[9,64,128]{2,1,0:T(8,128)}, f32[9,64,128]{2,1,0:T(8,128)}, f32[64,512]{1,0:T(8,128)}, f32[64,512]{1,0:T(8,12...) custom-call(s32[4]{0:T(128)S(1)} %copy-done.10, ...), custom_call_target="tpu_custom_call" | custom-call | flops 1 | bytes 4030468 | tf_op jit(solution)/shard_map/pallas_call | solution.py:412
  (151 shorter events, 54.2 us)
Async XLA Ops:
  3.4 11.2 %collective-permute-start.3 = (bf16[9,64,128]{2,1,0:T(8,128)(2,1)S(1)}, bf16[9,64,128]{2,1,0:T(8,128)(2,1)S(1)}, u32[]{:S(2)}, u32[]{:S(2)}) collective-permute-start(bf16[9,64,128]{2,1,0:T(8,128)(2,1)S(1)} %convert_element_type.201), channel_id=1, source_target_pairs={{0,8},{1,9},{2,10},{3,11},{4,12},{5,13},{6,14},{7,15},{8,0},{9,1},... | collective-permute-start | bytes 442376 | tf_op jit(solution)/shard_map/ppermute | solution.py:522
  8.1 16.3 %collective-permute-start = (bf16[1040,128]{1,0:T(8,128)(2,1)S(1)}, bf16[1040,128]{1,0:T(8,128)(2,1)S(1)}, u32[]{:S(2)}, u32[]{:S(2)}) collective-permute-start(bf16[1040,128]{1,0:T(8,128)(2,1)S(1)} %concatenate.29), channel_id=1, source_target_pairs={{0,1},{1,0},{2,3},{3,2},{4,5},{5,4},{6,7},{7,6},{8,9},{9,8},{10,11... | collective-permute-start | bytes 798728 | tf_op jit(solution)/shard_map/ppermute | solution.py:551
  8.1 16.3 %collective-permute-start.1 = (bf16[1040,128]{1,0:T(8,128)(2,1)S(1)}, bf16[1040,128]{1,0:T(8,128)(2,1)S(1)}, u32[]{:S(2)}, u32[]{:S(2)}) collective-permute-start(bf16[1040,128]{1,0:T(8,128)(2,1)S(1)} %concatenate.30), channel_id=1, source_target_pairs={{0,2},{1,3},{2,0},{3,1},{4,6},{5,7},{6,4},{7,5},{8,10},{9,11},{10,... | collective-permute-start | bytes 798728 | tf_op jit(solution)/shard_map/ppermute | solution.py:551
  8.6 15.8 %collective-permute-start.2 = (bf16[1040,128]{1,0:T(8,128)(2,1)S(1)}, bf16[1040,128]{1,0:T(8,128)(2,1)S(1)}, u32[]{:S(2)}, u32[]{:S(2)}) collective-permute-start(bf16[1040,128]{1,0:T(8,128)(2,1)S(1)} %concatenate.31), channel_id=1, source_target_pairs={{0,3},{1,2},{2,1},{3,0},{4,7},{5,6},{6,5},{7,4},{8,11},{9,10},{10,... | collective-permute-start | bytes 798728 | tf_op jit(solution)/shard_map/ppermute | solution.py:551
  12.0 12.4 %collective-permute-start.4 = (bf16[9,64,128]{2,1,0:T(8,128)(2,1)S(1)}, bf16[9,64,128]{2,1,0:T(8,128)(2,1)S(1)}, u32[]{:S(2)}, u32[]{:S(2)}) collective-permute-start(bf16[9,64,128]{2,1,0:T(8,128)(2,1)S(1)} %convert_element_type.201), channel_id=1, source_target_pairs={{0,16},{1,17},{2,18},{3,19},{4,20},{5,21},{6,22},{7,23},{8,24},{9,... | collective-permute-start | bytes 442376 | tf_op jit(solution)/shard_map/ppermute | solution.py:522
  14.6 9.8 %collective-permute-start.5 = (bf16[9,64,128]{2,1,0:T(8,128)(2,1)S(1)}, bf16[9,64,128]{2,1,0:T(8,128)(2,1)S(1)}, u32[]{:S(2)}, u32[]{:S(2)}) collective-permute-start(bf16[9,64,128]{2,1,0:T(8,128)(2,1)S(1)} %convert_element_type.201), channel_id=1, source_target_pairs={{0,24},{1,25},{2,26},{3,27},{4,28},{5,29},{6,30},{7,31},{8,16},{9,... | collective-permute-start | bytes 442376 | tf_op jit(solution)/shard_map/ppermute | solution.py:522
  24.5 15.8 %collective-permute-start.7 = (bf16[4,9,64,128]{3,2,1,0:T(8,128)(2,1)S(1)}, bf16[4,9,64,128]{3,2,1,0:T(8,128)(2,1)S(1)}, u32[]{:S(2)}, u32[]{:S(2)}) collective-permute-start(bf16[4,9,64,128]{3,2,1,0:T(8,128)(2,1)S(1)} %pad_maximum_fusion.1.refs_5_), channel_id=1, source_target_pairs={{0,4},{1,3},{2,6},{3,1},{4,0},{5,7},{6,2},{7,5},{8,12},{9,11},{10,... | collective-permute-start | bytes 1769480 | tf_op jit(solution)/shard_map/ppermute | solution.py:522
  26.1 14.3 %collective-permute-start.8 = (bf16[4,9,64,128]{3,2,1,0:T(8,128)(2,1)S(1)}, bf16[4,9,64,128]{3,2,1,0:T(8,128)(2,1)S(1)}, u32[]{:S(2)}, u32[]{:S(2)}) collective-permute-start(bf16[4,9,64,128]{3,2,1,0:T(8,128)(2,1)S(1)} %pad_maximum_fusion.1.refs_5_), channel_id=1, source_target_pairs={{0,2},{1,5},{2,0},{3,7},{4,6},{5,1},{6,4},{7,3},{8,10},{9,13},{10,... | collective-permute-start | bytes 1769480 | tf_op jit(solution)/shard_map/ppermute | solution.py:522
  28.0 12.0 %collective-permute-start.10 = (bf16[2,64,512]{2,1,0:T(8,128)(2,1)S(1)}, bf16[2,64,512]{2,1,0:T(8,128)(2,1)S(1)}, u32[]{:S(2)}, u32[]{:S(2)}) collective-permute-start(bf16[2,64,512]{2,1,0:T(8,128)(2,1)S(1)} %pad_maximum_fusion.6), channel_id=1, source_target_pairs={{0,16},{1,17},{2,18},{3,19},{4,20},{5,21},{6,22},{7,23},{8,24},{9,... | collective-permute-start | bytes 393224 | tf_op jit(solution)/shard_map/ppermute | solution.py:522
  40.3 16.1 %collective-permute-start.12 = (bf16[4,9,64,128]{3,2,1,0:T(8,128)(2,1)S(1)}, bf16[4,9,64,128]{3,2,1,0:T(8,128)(2,1)S(1)}, u32[]{:S(2)}, u32[]{:S(2)}) collective-permute-start(bf16[4,9,64,128]{3,2,1,0:T(8,128)(2,1)S(1)} %collective-permute-done.7.refs_6_), channel_id=1, source_target_pairs={{0,2},{1,5},{2,0},{3,7},{4,6},{5,1},{6,4},{7,3},{8,10},{9,13},{10,... | collective-permute-start | bytes 1769480 | tf_op jit(solution)/shard_map/ppermute | solution.py:522
  40.9 15.5 %collective-permute-start.13 = (bf16[4,2,64,512]{3,2,1,0:T(8,128)(2,1)S(1)}, bf16[4,2,64,512]{3,2,1,0:T(8,128)(2,1)S(1)}, u32[]{:S(2)}, u32[]{:S(2)}) collective-permute-start(bf16[4,2,64,512]{3,2,1,0:T(8,128)(2,1)S(1)} %pad_maximum_fusion.2.refs_8_), channel_id=1, source_target_pairs={{0,4},{1,5},{2,6},{3,7},{4,0},{5,1},{6,2},{7,3},{8,12},{9,13},{10,... | collective-permute-start | bytes 1572872 | tf_op jit(solution)/shard_map/ppermute | solution.py:522
  44.5 11.9 %collective-permute-start.15 = (bf16[2,64,512]{2,1,0:T(8,128)(2,1)S(1)}, bf16[2,64,512]{2,1,0:T(8,128)(2,1)S(1)}, u32[]{:S(2)}, u32[]{:S(2)}) collective-permute-start(bf16[2,64,512]{2,1,0:T(8,128)(2,1)S(1)} %pad_maximum_fusion.5), channel_id=1, source_target_pairs={{0,16},{1,17},{2,18},{3,19},{4,20},{5,21},{6,22},{7,23},{8,24},{9,... | collective-permute-start | bytes 393224 | tf_op jit(solution)/shard_map/ppermute | solution.py:522
  45.7 10.7 %collective-permute-start.16 = (bf16[2,64,512]{2,1,0:T(8,128)(2,1)S(1)}, bf16[2,64,512]{2,1,0:T(8,128)(2,1)S(1)}, u32[]{:S(2)}, u32[]{:S(2)}) collective-permute-start(bf16[2,64,512]{2,1,0:T(8,128)(2,1)S(1)} %pad_maximum_fusion.5), channel_id=1, source_target_pairs={{0,24},{1,25},{2,26},{3,27},{4,28},{5,29},{6,30},{7,31},{8,16},{9,... | collective-permute-start | bytes 393224 | tf_op jit(solution)/shard_map/ppermute | solution.py:522
  59.3 16.4 %collective-permute-start.22 = (bf16[4,2,64,512]{3,2,1,0:T(8,128)(2,1)S(1)}, bf16[4,2,64,512]{3,2,1,0:T(8,128)(2,1)S(1)}, u32[]{:S(2)}, u32[]{:S(2)}) collective-permute-start(bf16[4,2,64,512]{3,2,1,0:T(8,128)(2,1)S(1)} %pad_maximum_fusion.3.refs_12_), channel_id=1, source_target_pairs={{0,4},{1,5},{2,6},{3,7},{4,0},{5,1},{6,2},{7,3},{8,12},{9,13},{10,... | collective-permute-start | bytes 1572872 | tf_op jit(solution)/shard_map/ppermute | solution.py:522
  60.9 14.8 %collective-permute-start.23 = (bf16[4,2,64,512]{3,2,1,0:T(8,128)(2,1)S(1)}, bf16[4,2,64,512]{3,2,1,0:T(8,128)(2,1)S(1)}, u32[]{:S(2)}, u32[]{:S(2)}) collective-permute-start(bf16[4,2,64,512]{3,2,1,0:T(8,128)(2,1)S(1)} %pad_maximum_fusion.3.refs_12_), channel_id=1, source_target_pairs={{0,1},{1,0},{2,3},{3,2},{4,5},{5,4},{6,7},{7,6},{8,9},{9,8},{10,11... | collective-permute-start | bytes 1572872 | tf_op jit(solution)/shard_map/ppermute | solution.py:522
  61.2 14.5 %collective-permute-start.21 = (bf16[4,2,64,512]{3,2,1,0:T(8,128)(2,1)S(1)}, bf16[4,2,64,512]{3,2,1,0:T(8,128)(2,1)S(1)}, u32[]{:S(2)}, u32[]{:S(2)}) collective-permute-start(bf16[4,2,64,512]{3,2,1,0:T(8,128)(2,1)S(1)} %pad_maximum_fusion.2.refs_8_), channel_id=1, source_target_pairs={{0,1},{1,0},{2,3},{3,2},{4,5},{5,4},{6,7},{7,6},{8,9},{9,8},{10,11... | collective-permute-start | bytes 1572872 | tf_op jit(solution)/shard_map/ppermute | solution.py:522
  62.1 9.1 %collective-permute-start.24 = (bf16[1024,128]{1,0:T(8,128)(2,1)S(1)}, bf16[1024,128]{1,0:T(8,128)(2,1)S(1)}, u32[]{:S(2)}, u32[]{:S(2)}) collective-permute-start(bf16[1024,128]{1,0:T(8,128)(2,1)S(1)} %get-tuple-element.294), channel_id=1, source_target_pairs={{0,2},{1,3},{2,0},{3,1},{4,6},{5,7},{6,4},{7,5},{8,10},{9,11},{10,... | collective-permute-start | bytes 786440 | tf_op jit(solution)/shard_map/ppermute | solution.py:599
  62.9 12.8 %collective-permute-start.25 = (bf16[1024,128]{1,0:T(8,128)(2,1)S(1)}, bf16[1024,128]{1,0:T(8,128)(2,1)S(1)}, u32[]{:S(2)}, u32[]{:S(2)}) collective-permute-start(bf16[1024,128]{1,0:T(8,128)(2,1)S(1)} %get-tuple-element.293), channel_id=1, source_target_pairs={{0,3},{1,2},{2,1},{3,0},{4,7},{5,6},{6,5},{7,4},{8,11},{9,10},{10,... | collective-permute-start | bytes 786440 | tf_op jit(solution)/shard_map/ppermute | solution.py:599
  85.3 9.2 %collective-permute-start.30 = (bf16[1024,128]{1,0:T(8,128)(2,1)S(1)}, bf16[1024,128]{1,0:T(8,128)(2,1)S(1)}, u32[]{:S(2)}, u32[]{:S(2)}) collective-permute-start(bf16[1024,128]{1,0:T(8,128)(2,1)S(1)} %get-tuple-element.208), channel_id=1, source_target_pairs={{0,2},{1,3},{2,0},{3,1},{4,6},{5,7},{6,4},{7,5},{8,10},{9,11},{10,... | collective-permute-start | bytes 786440 | tf_op jit(solution)/shard_map/ppermute | solution.py:656
  102.7 14.8 %collective-permute-start.36 = (bf16[2,4,2,64,512]{4,3,2,1,0:T(8,128)(2,1)S(1)}, bf16[2,4,2,64,512]{4,3,2,1,0:T(8,128)(2,1)S(1)}, u32[]{:S(2)}, u32[]{:S(2)}) collective-permute-start(bf16[2,4,2,64,512]{4,3,2,1,0:T(8,128)(2,1)S(1)} %fusion), channel_id=1, source_target_pairs={{0,2},{1,5},{2,0},{3,7},{4,6},{5,1},{6,4},{7,3},{8,10},{9,13},{10,... | collective-permute-start | bytes 3145736 | tf_op jit(solution)/shard_map/ppermute | solution.py:522
  118.8 21.9 %collective-permute-start.37 = (bf16[2,4,9,64,128]{4,3,2,1,0:T(8,128)(2,1)S(1)}, bf16[2,4,9,64,128]{4,3,2,1,0:T(8,128)(2,1)S(1)}, u32[]{:S(2)}, u32[]{:S(2)}) collective-permute-start(bf16[2,4,9,64,128]{4,3,2,1,0:T(8,128)(2,1)S(1)} %get-tuple-element.240), channel_id=1, source_target_pairs={{0,2},{1,5},{2,0},{3,7},{4,6},{5,1},{6,4},{7,3},{8,10},{9,13},{10,... | collective-permute-start | bytes 3538952 | tf_op jit(solution)/shard_map/ppermute | solution.py:522
  120.3 22.1 %collective-permute-start.45 = (bf16[4,2,64,512]{3,2,1,0:T(8,128)(2,1)S(1)}, bf16[4,2,64,512]{3,2,1,0:T(8,128)(2,1)S(1)}, u32[]{:S(2)}, u32[]{:S(2)}) collective-permute-start(bf16[4,2,64,512]{3,2,1,0:T(8,128)(2,1)S(1)} %fusion.1), channel_id=1, source_target_pairs={{0,4},{1,3},{2,6},{3,1},{4,0},{5,7},{6,2},{7,5},{8,12},{9,11},{10,... | collective-permute-start | bytes 1572872 | tf_op jit(solution)/shard_map/ppermute | solution.py:522
  140.8 11.3 %collective-permute-start.38 = (bf16[4,9,64,128]{3,2,1,0:T(8,128)(2,1)S(1)}, bf16[4,9,64,128]{3,2,1,0:T(8,128)(2,1)S(1)}, u32[]{:S(2)}, u32[]{:S(2)}) collective-permute-start(bf16[4,9,64,128]{3,2,1,0:T(8,128)(2,1)S(1)} %fusion.2), channel_id=1, source_target_pairs={{0,4},{1,3},{2,6},{3,1},{4,0},{5,7},{6,2},{7,5},{8,12},{9,11},{10,... | collective-permute-start | bytes 1769480 | tf_op jit(solution)/shard_map/ppermute | solution.py:522
  142.4 10.2 %collective-permute-start.42 = (bf16[1024,128]{1,0:T(8,128)(2,1)S(1)}, bf16[1024,128]{1,0:T(8,128)(2,1)S(1)}, u32[]{:S(2)}, u32[]{:S(2)}) collective-permute-start(bf16[1024,128]{1,0:T(8,128)(2,1)S(1)} %get-tuple-element.245), channel_id=1, source_target_pairs={{0,1},{1,0},{2,3},{3,2},{4,5},{5,4},{6,7},{7,6},{8,9},{9,8},{10,11... | collective-permute-start | bytes 786440 | tf_op jit(solution)/shard_map/ppermute | solution.py:723
  142.7 12.7 %collective-permute-start.46 = (bf16[2,64,512]{2,1,0:T(8,128)(2,1)S(1)}, bf16[2,64,512]{2,1,0:T(8,128)(2,1)S(1)}, u32[]{:S(2)}, u32[]{:S(2)}) collective-permute-start(bf16[2,64,512]{2,1,0:T(8,128)(2,1)S(1)} %get-tuple-element.278), channel_id=1, source_target_pairs={{0,8},{1,9},{2,10},{3,11},{4,12},{5,13},{6,14},{7,15},{8,0},{9,1},... | collective-permute-start | bytes 393224 | tf_op jit(solution)/shard_map/ppermute | solution.py:522
  149.3 12.9 %collective-permute-start.47 = (bf16[2,64,512]{2,1,0:T(8,128)(2,1)S(1)}, bf16[2,64,512]{2,1,0:T(8,128)(2,1)S(1)}, u32[]{:S(2)}, u32[]{:S(2)}) collective-permute-start(bf16[2,64,512]{2,1,0:T(8,128)(2,1)S(1)} %get-tuple-element.280), channel_id=1, source_target_pairs={{0,16},{1,17},{2,18},{3,19},{4,20},{5,21},{6,22},{7,23},{8,24},{9,... | collective-permute-start | bytes 393224 | tf_op jit(solution)/shard_map/ppermute | solution.py:522
  151.7 10.6 %collective-permute-start.48 = (bf16[2,64,512]{2,1,0:T(8,128)(2,1)S(1)}, bf16[2,64,512]{2,1,0:T(8,128)(2,1)S(1)}, u32[]{:S(2)}, u32[]{:S(2)}) collective-permute-start(bf16[2,64,512]{2,1,0:T(8,128)(2,1)S(1)} %get-tuple-element.279), channel_id=1, source_target_pairs={{0,24},{1,25},{2,26},{3,27},{4,28},{5,29},{6,30},{7,31},{8,16},{9,... | collective-permute-start | bytes 393224 | tf_op jit(solution)/shard_map/ppermute | solution.py:522
  152.1 23.5 %collective-permute-start.43 = (bf16[1024,128]{1,0:T(8,128)(2,1)S(1)}, bf16[1024,128]{1,0:T(8,128)(2,1)S(1)}, u32[]{:S(2)}, u32[]{:S(2)}) collective-permute-start(bf16[1024,128]{1,0:T(8,128)(2,1)S(1)} %get-tuple-element.246), channel_id=1, source_target_pairs={{0,2},{1,3},{2,0},{3,1},{4,6},{5,7},{6,4},{7,5},{8,10},{9,11},{10,... | collective-permute-start | bytes 786440 | tf_op jit(solution)/shard_map/ppermute | solution.py:723
  152.7 23.0 %collective-permute-start.44 = (bf16[1024,128]{1,0:T(8,128)(2,1)S(1)}, bf16[1024,128]{1,0:T(8,128)(2,1)S(1)}, u32[]{:S(2)}, u32[]{:S(2)}) collective-permute-start(bf16[1024,128]{1,0:T(8,128)(2,1)S(1)} %get-tuple-element.247), channel_id=1, source_target_pairs={{0,3},{1,2},{2,1},{3,0},{4,7},{5,6},{6,5},{7,4},{8,11},{9,10},{10,... | collective-permute-start | bytes 786440 | tf_op jit(solution)/shard_map/ppermute | solution.py:723
  155.3 10.9 %collective-permute-start.39 = (bf16[9,64,128]{2,1,0:T(8,128)(2,1)S(1)}, bf16[9,64,128]{2,1,0:T(8,128)(2,1)S(1)}, u32[]{:S(2)}, u32[]{:S(2)}) collective-permute-start(bf16[9,64,128]{2,1,0:T(8,128)(2,1)S(1)} %get-tuple-element.283), channel_id=1, source_target_pairs={{0,8},{1,9},{2,10},{3,11},{4,12},{5,13},{6,14},{7,15},{8,0},{9,1},... | collective-permute-start | bytes 442376 | tf_op jit(solution)/shard_map/ppermute | solution.py:522
  162.3 13.4 %collective-permute-start.40 = (bf16[9,64,128]{2,1,0:T(8,128)(2,1)S(1)}, bf16[9,64,128]{2,1,0:T(8,128)(2,1)S(1)}, u32[]{:S(2)}, u32[]{:S(2)}) collective-permute-start(bf16[9,64,128]{2,1,0:T(8,128)(2,1)S(1)} %get-tuple-element.282), channel_id=1, source_target_pairs={{0,16},{1,17},{2,18},{3,19},{4,20},{5,21},{6,22},{7,23},{8,24},{9,... | collective-permute-start | bytes 442376 | tf_op jit(solution)/shard_map/ppermute | solution.py:522
  162.3 13.4 %collective-permute-start.41 = (bf16[9,64,128]{2,1,0:T(8,128)(2,1)S(1)}, bf16[9,64,128]{2,1,0:T(8,128)(2,1)S(1)}, u32[]{:S(2)}, u32[]{:S(2)}) collective-permute-start(bf16[9,64,128]{2,1,0:T(8,128)(2,1)S(1)} %get-tuple-element.281), channel_id=1, source_target_pairs={{0,24},{1,25},{2,26},{3,27},{4,28},{5,29},{6,30},{7,31},{8,16},{9,... | collective-permute-start | bytes 442376 | tf_op jit(solution)/shard_map/ppermute | solution.py:522
  (39 other events, 280.3 us)
where the time goes:
time: 198 us; the launch traced here: 197 us
  waiting for transfers between devices  91.5 us (46%)
  starting transfers between devices  66.7 us (34%)
  Pallas kernels  30.2 us (15%)
  other arithmetic  5.18 us (3%)
  local copies, waits for them, and re-layouts  2.15 us (1%)
    ppermute x42, waiting for transfers between devices, send(): return lax.ppermute(values, axes, pairs)  76.9 us
    ppermute x42, starting transfers between devices, send(): return lax.ppermute(values, axes, pairs)  57.7 us
    pallas_call x9, Pallas kernels, call(): pl.pallas_call(placed(kernel), out_shape=outs, in_specs=[pl.BlockSpec(mem...  30.2 us
    ppermute x2, waiting for transfers between devices, per_device(): lax.ppermute(c_blocks[k], 'mp', within[k])  7.42 us
  transfers between devices with their start and end apart: 54, of which 26 were waited for; matrix products, arithmetic and copies ran while one was open for 2% of the time, Pallas kernels for 10%

commit v1 on v0

--- a/solution.py
+++ b/solution.py
@@ -246,13 +246,13 @@
         second = (s * vec[3:4, :] + vec[4:5, :]).astype(bf16)
         sec[rows, :] = second
         grad = mg[rows, :]
-        for j in range(hidden // 512):
-            cols = slice(j * 512, (j + 1) * 512)
+        for j in range(hidden // ROWS):
+            cols = slice(j * ROWS, (j + 1) * ROWS)
+            back = dot(grad, wo[:, cols])
             h = dot(second, wh[:, cols]) + hbias[0:1, cols]
             phi = phi_of(h)
             act[rows, cols] = (h * phi).astype(bf16)
-            hidden_grad = (dot(grad, wo[:, cols]) * slope_of(h, phi)).astype(bf16)
-            hg[rows, cols] = hidden_grad
+            hg[rows, cols] = (back * slope_of(h, phi)).astype(bf16)
         mixed = dot(act[rows, :], wo[...], NT)
         values_ref[...] = (residual + (mixed + vec[5:6, :])).astype(bf16)
         store_columns(place, outs, rows, values_ref)

time: 198 us -> 198 us (level)
  starting transfers between devices: 66.7 us -> 61.6 us
  waiting for transfers between devices: 91.5 us -> 96.4 us
    ppermute x42, waiting for transfers between devices: 76.9 us -> 80.5 us  [send(): return lax.ppermute(values, axes, pairs)]
    ppermute x2, starting transfers between devices: 3.09 us -> 0.75 us  [per_device(): block_parts[k] = lax.ppermute(block_parts[k], 'mp', within[k])]
where the time goes in v1:
time: 198 us; the launch traced here: 197 us
  waiting for transfers between devices  96.4 us (49%)
  starting transfers between devices  61.6 us (31%)
  Pallas kernels  30 us (15%)
  other arithmetic  5.18 us (3%)
  local copies, waits for them, and re-layouts  2.15 us (1%)
    ppermute x42, waiting for transfers between devices, send(): return lax.ppermute(values, axes, pairs)  80.5 us
    ppermute x42, starting transfers between devices, send(): return lax.ppermute(values, axes, pairs)  55.7 us
    pallas_call x9, Pallas kernels, call(): pl.pallas_call(placed(kernel), out_shape=outs, in_specs=[pl.BlockSpec(mem...  30 us
    ppermute x2, waiting for transfers between devices, per_device(): lax.ppermute(c_blocks[k], 'mp', within[k])  7.42 us
  transfers between devices with their start and end apart: 54, of which 26 were waited for; matrix products, arithmetic and copies ran while one was open for 2% of the time, Pallas kernels for 10%

profile of v1, /device:TPU:0, one launch (start us, length us, event | category | flops | bytes accessed | tf_op | source)
XLA Modules:
  0.0 196.7 jit_solution(9871506319649542057)
XLA Ops:
  3.4 3.1 %collective-permute-start.3 = (bf16[9,64,128]{2,1,0:T(8,128)(2,1)S(1)}, bf16[9,64,128]{2,1,0:T(8,128)(2,1)S(1)}, u32[]{:S(2)}, u32[]{:S(2)}) collective-permute-start(bf16[9,64,128]{2,1,0:T(8,128)(2,1)S(1)} %convert_element_type.201), channel_id=1, source_target_pairs={{0,8},{1,9},{2,10},{3,11},{4,12},{5,13},{6,14},{7,15},{8,0},{9,1},... | collective-permute-start | bytes 442376 | tf_op jit(solution)/shard_map/ppermute | solution.py:522
  10.0 2.0 %collective-permute-done.6 = bf16[2,64,512]{2,1,0:T(8,128)(2,1)S(1)} collective-permute-done((bf16[2,64,512]{2,1,0:T(8,128)(2,1)S(1)}, bf16[2,64,512]{2,1,0:T(8,128)(2,1)S(1)}, u32[]{:S(2)}, u32[]{:S(2)}) %collective-permute-start.6) | collective-permute-done | bytes 131104 | tf_op jit(solution)/shard_map/ppermute | solution.py:522
  12.0 2.6 %collective-permute-start.4 = (bf16[9,64,128]{2,1,0:T(8,128)(2,1)S(1)}, bf16[9,64,128]{2,1,0:T(8,128)(2,1)S(1)}, u32[]{:S(2)}, u32[]{:S(2)}) collective-permute-start(bf16[9,64,128]{2,1,0:T(8,128)(2,1)S(1)} %convert_element_type.201), channel_id=1, source_target_pairs={{0,16},{1,17},{2,18},{3,19},{4,20},{5,21},{6,22},{7,23},{8,24},{9,... | collective-permute-start | bytes 442376 | tf_op jit(solution)/shard_map/ppermute | solution.py:522
  14.9 9.5 %collective-permute-done.4 = bf16[9,64,128]{2,1,0:T(8,128)(2,1)S(1)} collective-permute-done((bf16[9,64,128]{2,1,0:T(8,128)(2,1)S(1)}, bf16[9,64,128]{2,1,0:T(8,128)(2,1)S(1)}, u32[]{:S(2)}, u32[]{:S(2)}) %collective-permute-start.4) | collective-permute-done | bytes 147488 | tf_op jit(solution)/shard_map/ppermute | solution.py:522
  26.1 1.9 collective-permute-start.8
  28.0 3.3 %collective-permute-start.10 = (bf16[2,64,512]{2,1,0:T(8,128)(2,1)S(1)}, bf16[2,64,512]{2,1,0:T(8,128)(2,1)S(1)}, u32[]{:S(2)}, u32[]{:S(2)}) collective-permute-start(bf16[2,64,512]{2,1,0:T(8,128)(2,1)S(1)} %pad_maximum_fusion.6), channel_id=1, source_target_pairs={{0,16},{1,17},{2,18},{3,19},{4,20},{5,21},{6,22},{7,23},{8,24},{9,... | collective-permute-start | bytes 393224 | tf_op jit(solution)/shard_map/ppermute | solution.py:522
  32.5 7.4 %collective-permute-done.10 = bf16[2,64,512]{2,1,0:T(8,128)(2,1)S(1)} collective-permute-done((bf16[2,64,512]{2,1,0:T(8,128)(2,1)S(1)}, bf16[2,64,512]{2,1,0:T(8,128)(2,1)S(1)}, u32[]{:S(2)}, u32[]{:S(2)}) %collective-permute-start.10) | collective-permute-done | bytes 131104 | tf_op jit(solution)/shard_map/ppermute | solution.py:522
  41.9 2.6 %collective-permute-start.14 = (bf16[2,64,512]{2,1,0:T(8,128)(2,1)S(1)}, bf16[2,64,512]{2,1,0:T(8,128)(2,1)S(1)}, u32[]{:S(2)}, u32[]{:S(2)}) collective-permute-start(bf16[2,64,512]{2,1,0:T(8,128)(2,1)S(1)} %pad_maximum_fusion.5), channel_id=1, source_target_pairs={{0,8},{1,9},{2,10},{3,11},{4,12},{5,13},{6,14},{7,15},{8,0},{9,1},... | collective-permute-start | bytes 393224 | tf_op jit(solution)/shard_map/ppermute | solution.py:522
  48.9 7.5 %collective-permute-done.15 = bf16[2,64,512]{2,1,0:T(8,128)(2,1)S(1)} collective-permute-done((bf16[2,64,512]{2,1,0:T(8,128)(2,1)S(1)}, bf16[2,64,512]{2,1,0:T(8,128)(2,1)S(1)}, u32[]{:S(2)}, u32[]{:S(2)}) %collective-permute-start.15) | collective-permute-done | bytes 131104 | tf_op jit(solution)/shard_map/ppermute | solution.py:522
  56.4 2.4 %collective-permute-start.17 = (bf16[4,9,64,128]{3,2,1,0:T(8,128)(2,1)S(1)}, bf16[4,9,64,128]{3,2,1,0:T(8,128)(2,1)S(1)}, u32[]{:S(2)}, u32[]{:S(2)}) collective-permute-start(bf16[4,9,64,128]{3,2,1,0:T(8,128)(2,1)S(1)} %pad_maximum_fusion.1.refs_5_), channel_id=1, source_target_pairs={{0,1},{1,0},{2,3},{3,2},{4,5},{5,4},{6,7},{7,6},{8,9},{9,8},{10,11... | collective-permute-start | bytes 1769480 | tf_op jit(solution)/shard_map/ppermute | solution.py:522
  63.8 4.5 %shard_map.313 = (bf16[9,512,512]{2,1,0:T(8,128)(2,1)S(1)}, bf16[1024,512]{1,0:T(8,128)(2,1)S(1)}, bf16[1024,512]{1,0:T(8,128)(2,1)S(1)}, f32[1024,512]{1,0:T(8,...) custom-call(s32[4]{0:T(128)S(1)} %copy-done.10, bf16[1040,128]{1,0:T(8,128)(2,1)S(1)} %concatenate.28.refs_0_, ...), custom_call_target="tpu_custom_call" | custom-call | flops 4831838208 | bytes 16814080 | tf_op jit(solution)/shard_map/pallas_call | solution.py:412
  68.3 2.9 %collective-permute-done.24.refs_4_ = bf16[1024,128]{1,0:T(8,128)(2,1)S(1)} collective-permute-done((bf16[1024,128]{1,0:T(8,128)(2,1)S(1)}, bf16[1024,128]{1,0:T(8,128)(2,1)S(1)}, u32[]{:S(2)}, u32[]{:S(2)}) %collective-permute-start.24) | collective-permute-done | bytes 262176 | tf_op jit(solution)/shard_map/ppermute | solution.py:599
  71.2 4.5 %collective-permute-done.25.refs_5_ = bf16[1024,128]{1,0:T(8,128)(2,1)S(1)} collective-permute-done((bf16[1024,128]{1,0:T(8,128)(2,1)S(1)}, bf16[1024,128]{1,0:T(8,128)(2,1)S(1)}, u32[]{:S(2)}, u32[]{:S(2)}) %collective-permute-start.25) | collective-permute-done | bytes 262176 | tf_op jit(solution)/shard_map/ppermute | solution.py:599
  76.7 2.2 %collective-permute-done.26.refs_3_ = bf16[1024,128]{1,0:T(8,128)(2,1)S(1)} collective-permute-done((bf16[1024,128]{1,0:T(8,128)(2,1)S(1)}, bf16[1024,128]{1,0:T(8,128)(2,1)S(1)}, u32[]{:S(2)}, u32[]{:S(2)}) %collective-permute-start.26) | collective-permute-done | bytes 262176 | tf_op jit(solution)/shard_map/ppermute | solution.py:631
  78.8 5.8 %shard_map.314 = (bf16[1024,128]{1,0:T(8,128)(2,1)S(1)}, bf16[1024,128]{1,0:T(8,128)(2,1)S(1)}, bf16[1024,128]{1,0:T(8,128)(2,1)S(1)}, bf16[1024,128]{1,0:T(8,12...) custom-call(s32[4]{0:T(128)S(1)} %copy-done.10, ...), custom_call_target="tpu_custom_call" | custom-call | flops 6442450944 | bytes 22040576 | tf_op jit(solution)/shard_map/pallas_call | solution.py:412
  85.4 5.2 %shard_map.315 = (bf16[2,2,4,2,64,512]{5,4,3,2,1,0:T(8,128)(2,1)S(1)}, bf16[2,2,4,2,64,512]{5,4,3,2,1,0:T(8,128)(2,1)S(1)}, f32[1,2048]{1,0:T(1,128)S(1)}) custom-call(s32[4]{0:T(128)S(1)} %copy-done.10, bf16[1024,512]{1,0:T(8,128)(2,1)S(1)} %get-tuple-element.201.refs_0_, bf16[1024,2048]{1,0:T(8,128)(2,1)S(1)} %get-tuple-element.213.refs_1_.refs_3_, ...), custom_call_target="tpu_custom_call" | custom-call | flops 1 | bytes 14688256 | tf_op jit(solution)/shard_map/pallas_call | solution.py:412
  90.6 2.9 %collective-permute-done.30 = bf16[1024,128]{1,0:T(8,128)(2,1)S(1)} collective-permute-done((bf16[1024,128]{1,0:T(8,128)(2,1)S(1)}, bf16[1024,128]{1,0:T(8,128)(2,1)S(1)}, u32[]{:S(2)}, u32[]{:S(2)}) %collective-permute-start.30) | collective-permute-done | bytes 262176 | tf_op jit(solution)/shard_map/ppermute | solution.py:656
  98.0 3.4 %collective-permute-done.32 = bf16[1024,128]{1,0:T(8,128)(2,1)S(1)} collective-permute-done((bf16[1024,128]{1,0:T(8,128)(2,1)S(1)}, bf16[1024,128]{1,0:T(8,128)(2,1)S(1)}, u32[]{:S(2)}, u32[]{:S(2)}) %collective-permute-start.32) | collective-permute-done | bytes 262176 | tf_op jit(solution)/shard_map/ppermute | solution.py:670
  102.0 5.9 %shard_map.317 = (bf16[2,2,4,9,64,128]{5,4,3,2,1,0:T(8,128)(2,1)S(1)}, bf16[2,2,4,3,64,128]{5,4,3,2,1,0:T(8,128)(2,1)S(1)}, bf16[2,2,4,3,64,128]{5,4,3,2,1,0:T(8...) custom-call(s32[4]{0:T(128)S(1)} %copy-done.10, bf16[1024,512]{1,0:T(8,128)(2,1)S(1)} %get-tuple-element.221.refs_0_, ...), custom_call_target="tpu_custom_call" | custom-call | flops 1 | bytes 7995392 | tf_op jit(solution)/shard_map/pallas_call | solution.py:412
  109.6 2.7 %shard_map.318 = (bf16[1024,128]{1,0:T(8,128)(2,1)S(1)}, bf16[1024,128]{1,0:T(8,128)(2,1)S(1)}, bf16[1024,128]{1,0:T(8,128)(2,1)S(1)}, bf16[1024,128]{1,0:T(8,128)(2,1)S(1)}, f32[8,512]{1,0:T(8,128)S(1)}) custom-call(s32[4]{0:T(128)S(1)} %copy-done.10, bf16[1024,512]{1,0:T(8,128)(2,1)S(1)} %get-tuple-element.183.refs_0_, ...), custom_call_target="tpu_custom_call" | custom-call | flops 1 | bytes 11169792 | tf_op jit(solution)/shard_map/pallas_call | solution.py:412
  112.3 3.9 %collective-permute-done.36 = bf16[2,4,2,64,512]{4,3,2,1,0:T(8,128)(2,1)S(1)} collective-permute-done((bf16[2,4,2,64,512]{4,3,2,1,0:T(8,128)(2,1)S(1)}, bf16[2,4,2,64,512]{4,3,2,1,0:T(8,128)(2,1)S(1)}, u32[]{:S(2)}, u32[]{:S(2)}) %collective-permute-start.36) | collective-permute-done | bytes 1048608 | tf_op jit(solution)/shard_map/ppermute | solution.py:522
  119.6 19.6 %collective-permute-done.37 = bf16[2,4,9,64,128]{4,3,2,1,0:T(8,128)(2,1)S(1)} collective-permute-done((bf16[2,4,9,64,128]{4,3,2,1,0:T(8,128)(2,1)S(1)}, bf16[2,4,9,64,128]{4,3,2,1,0:T(8,128)(2,1)S(1)}, u32[]{:S(2)}, u32[]{:S(2)}) %collective-permute-start.37) | collective-permute-done | bytes 1179680 | tf_op jit(solution)/shard_map/ppermute | solution.py:522
  140.3 9.0 %collective-permute-start.46 = (bf16[2,64,512]{2,1,0:T(8,128)(2,1)S(1)}, bf16[2,64,512]{2,1,0:T(8,128)(2,1)S(1)}, u32[]{:S(2)}, u32[]{:S(2)}) collective-permute-start(bf16[2,64,512]{2,1,0:T(8,128)(2,1)S(1)} %get-tuple-element.278), channel_id=1, source_target_pairs={{0,8},{1,9},{2,10},{3,11},{4,12},{5,13},{6,14},{7,15},{8,0},{9,1},... | collective-permute-start | bytes 393224 | tf_op jit(solution)/shard_map/ppermute | solution.py:522
  153.4 2.2 %collective-permute-done.46 = bf16[2,64,512]{2,1,0:T(8,128)(2,1)S(1)} collective-permute-done((bf16[2,64,512]{2,1,0:T(8,128)(2,1)S(1)}, bf16[2,64,512]{2,1,0:T(8,128)(2,1)S(1)}, u32[]{:S(2)}, u32[]{:S(2)}) %collective-permute-start.46) | collective-permute-done | bytes 131104 | tf_op jit(solution)/shard_map/ppermute | solution.py:522
  155.6 2.1 %collective-permute-start.39 = (bf16[9,64,128]{2,1,0:T(8,128)(2,1)S(1)}, bf16[9,64,128]{2,1,0:T(8,128)(2,1)S(1)}, u32[]{:S(2)}, u32[]{:S(2)}) collective-permute-start(bf16[9,64,128]{2,1,0:T(8,128)(2,1)S(1)} %get-tuple-element.283), channel_id=1, source_target_pairs={{0,8},{1,9},{2,10},{3,11},{4,12},{5,13},{6,14},{7,15},{8,0},{9,1},... | collective-permute-start | bytes 442376 | tf_op jit(solution)/shard_map/ppermute | solution.py:522
  157.7 4.5 %collective-permute-done.47 = bf16[2,64,512]{2,1,0:T(8,128)(2,1)S(1)} collective-permute-done((bf16[2,64,512]{2,1,0:T(8,128)(2,1)S(1)}, bf16[2,64,512]{2,1,0:T(8,128)(2,1)S(1)}, u32[]{:S(2)}, u32[]{:S(2)}) %collective-permute-start.47) | collective-permute-done | bytes 131104 | tf_op jit(solution)/shard_map/ppermute | solution.py:522
  162.2 2.2 %collective-permute-start.41 = (bf16[9,64,128]{2,1,0:T(8,128)(2,1)S(1)}, bf16[9,64,128]{2,1,0:T(8,128)(2,1)S(1)}, u32[]{:S(2)}, u32[]{:S(2)}) collective-permute-start(bf16[9,64,128]{2,1,0:T(8,128)(2,1)S(1)} %get-tuple-element.281), channel_id=1, source_target_pairs={{0,24},{1,25},{2,26},{3,27},{4,28},{5,29},{6,30},{7,31},{8,16},{9,... | collective-permute-start | bytes 442376 | tf_op jit(solution)/shard_map/ppermute | solution.py:522
  166.1 9.1 %collective-permute-done.40.refs_2_ = bf16[9,64,128]{2,1,0:T(8,128)(2,1)S(1)} collective-permute-done((bf16[9,64,128]{2,1,0:T(8,128)(2,1)S(1)}, bf16[9,64,128]{2,1,0:T(8,128)(2,1)S(1)}, u32[]{:S(2)}, u32[]{:S(2)}) %collective-permute-start.40) | collective-permute-done | bytes 147488 | tf_op jit(solution)/shard_map/ppermute | solution.py:522
  177.4 2.2 %collective-permute-start.50 = (f32[11,512]{1,0:T(8,128)S(1)}, f32[11,512]{1,0:T(8,128)S(1)}, u32[]{:S(2)}, u32[]{:S(2)}) collective-permute-start(f32[11,512]{1,0:T(8,128)S(1)} %add.179), channel_id=1, source_target_pairs={{0,8},{1,9},{2,10},{3,11},{4,12},{5,13},{6,14},{7,15},{8,0},{9,1},... | collective-permute-start | bytes 67592 | tf_op jit(solution)/shard_map/ppermute | solution.py:522
  181.5 2.7 %collective-permute-start.51 = (f32[11,512]{1,0:T(8,128)S(1)}, f32[11,512]{1,0:T(8,128)S(1)}, u32[]{:S(2)}, u32[]{:S(2)}) collective-permute-start(f32[11,512]{1,0:T(8,128)S(1)} %add.180), channel_id=1, source_target_pairs={{0,16},{1,17},{2,18},{3,19},{4,20},{5,21},{6,22},{7,23},{8,24},{9,... | collective-permute-start | bytes 67592 | tf_op jit(solution)/shard_map/ppermute | solution.py:522
  187.3 2.9 %collective-permute-done.52 = f32[11,512]{1,0:T(8,128)S(1)} collective-permute-done((f32[11,512]{1,0:T(8,128)S(1)}, f32[11,512]{1,0:T(8,128)S(1)}, u32[]{:S(2)}, u32[]{:S(2)}) %collective-permute-start.52) | collective-permute-done | bytes 22560 | tf_op jit(solution)/shard_map/ppermute | solution.py:522
  194.2 2.3 %shard_map.321 = (f32[9,64,128]{2,1,0:T(8,128)}, f32[9,64,128]{2,1,0:T(8,128)}, f32[9,64,128]{2,1,0:T(8,128)}, f32[64,512]{1,0:T(8,128)}, f32[64,512]{1,0:T(8,12...) custom-call(s32[4]{0:T(128)S(1)} %copy-done.10, ...), custom_call_target="tpu_custom_call" | custom-call | flops 1 | bytes 4030468 | tf_op jit(solution)/shard_map/pallas_call | solution.py:412
  (151 shorter events, 50.4 us)
Async XLA Ops:
  3.4 11.2 %collective-permute-start.3 = (bf16[9,64,128]{2,1,0:T(8,128)(2,1)S(1)}, bf16[9,64,128]{2,1,0:T(8,128)(2,1)S(1)}, u32[]{:S(2)}, u32[]{:S(2)}) collective-permute-start(bf16[9,64,128]{2,1,0:T(8,128)(2,1)S(1)} %convert_element_type.201), channel_id=1, source_target_pairs={{0,8},{1,9},{2,10},{3,11},{4,12},{5,13},{6,14},{7,15},{8,0},{9,1},... | collective-permute-start | bytes 442376 | tf_op jit(solution)/shard_map/ppermute | solution.py:522
  8.1 16.3 %collective-permute-start = (bf16[1040,128]{1,0:T(8,128)(2,1)S(1)}, bf16[1040,128]{1,0:T(8,128)(2,1)S(1)}, u32[]{:S(2)}, u32[]{:S(2)}) collective-permute-start(bf16[1040,128]{1,0:T(8,128)(2,1)S(1)} %concatenate.29), channel_id=1, source_target_pairs={{0,1},{1,0},{2,3},{3,2},{4,5},{5,4},{6,7},{7,6},{8,9},{9,8},{10,11... | collective-permute-start | bytes 798728 | tf_op jit(solution)/shard_map/ppermute | solution.py:551
  8.1 16.3 %collective-permute-start.1 = (bf16[1040,128]{1,0:T(8,128)(2,1)S(1)}, bf16[1040,128]{1,0:T(8,128)(2,1)S(1)}, u32[]{:S(2)}, u32[]{:S(2)}) collective-permute-start(bf16[1040,128]{1,0:T(8,128)(2,1)S(1)} %concatenate.30), channel_id=1, source_target_pairs={{0,2},{1,3},{2,0},{3,1},{4,6},{5,7},{6,4},{7,5},{8,10},{9,11},{10,... | collective-permute-start | bytes 798728 | tf_op jit(solution)/shard_map/ppermute | solution.py:551
  8.6 15.8 %collective-permute-start.2 = (bf16[1040,128]{1,0:T(8,128)(2,1)S(1)}, bf16[1040,128]{1,0:T(8,128)(2,1)S(1)}, u32[]{:S(2)}, u32[]{:S(2)}) collective-permute-start(bf16[1040,128]{1,0:T(8,128)(2,1)S(1)} %concatenate.31), channel_id=1, source_target_pairs={{0,3},{1,2},{2,1},{3,0},{4,7},{5,6},{6,5},{7,4},{8,11},{9,10},{10,... | collective-permute-start | bytes 798728 | tf_op jit(solution)/shard_map/ppermute | solution.py:551
  12.0 12.4 %collective-permute-start.4 = (bf16[9,64,128]{2,1,0:T(8,128)(2,1)S(1)}, bf16[9,64,128]{2,1,0:T(8,128)(2,1)S(1)}, u32[]{:S(2)}, u32[]{:S(2)}) collective-permute-start(bf16[9,64,128]{2,1,0:T(8,128)(2,1)S(1)} %convert_element_type.201), channel_id=1, source_target_pairs={{0,16},{1,17},{2,18},{3,19},{4,20},{5,21},{6,22},{7,23},{8,24},{9,... | collective-permute-start | bytes 442376 | tf_op jit(solution)/shard_map/ppermute | solution.py:522
  14.6 9.8 %collective-permute-start.5 = (bf16[9,64,128]{2,1,0:T(8,128)(2,1)S(1)}, bf16[9,64,128]{2,1,0:T(8,128)(2,1)S(1)}, u32[]{:S(2)}, u32[]{:S(2)}) collective-permute-start(bf16[9,64,128]{2,1,0:T(8,128)(2,1)S(1)} %convert_element_type.201), channel_id=1, source_target_pairs={{0,24},{1,25},{2,26},{3,27},{4,28},{5,29},{6,30},{7,31},{8,16},{9,... | collective-permute-start | bytes 442376 | tf_op jit(solution)/shard_map/ppermute | solution.py:522
  24.5 15.8 %collective-permute-start.7 = (bf16[4,9,64,128]{3,2,1,0:T(8,128)(2,1)S(1)}, bf16[4,9,64,128]{3,2,1,0:T(8,128)(2,1)S(1)}, u32[]{:S(2)}, u32[]{:S(2)}) collective-permute-start(bf16[4,9,64,128]{3,2,1,0:T(8,128)(2,1)S(1)} %pad_maximum_fusion.1.refs_5_), channel_id=1, source_target_pairs={{0,4},{1,3},{2,6},{3,1},{4,0},{5,7},{6,2},{7,5},{8,12},{9,11},{10,... | collective-permute-start | bytes 1769480 | tf_op jit(solution)/shard_map/ppermute | solution.py:522
  26.1 14.3 %collective-permute-start.8 = (bf16[4,9,64,128]{3,2,1,0:T(8,128)(2,1)S(1)}, bf16[4,9,64,128]{3,2,1,0:T(8,128)(2,1)S(1)}, u32[]{:S(2)}, u32[]{:S(2)}) collective-permute-start(bf16[4,9,64,128]{3,2,1,0:T(8,128)(2,1)S(1)} %pad_maximum_fusion.1.refs_5_), channel_id=1, source_target_pairs={{0,2},{1,5},{2,0},{3,7},{4,6},{5,1},{6,4},{7,3},{8,10},{9,13},{10,... | collective-permute-start | bytes 1769480 | tf_op jit(solution)/shard_map/ppermute | solution.py:522
  28.0 12.0 %collective-permute-start.10 = (bf16[2,64,512]{2,1,0:T(8,128)(2,1)S(1)}, bf16[2,64,512]{2,1,0:T(8,128)(2,1)S(1)}, u32[]{:S(2)}, u32[]{:S(2)}) collective-permute-start(bf16[2,64,512]{2,1,0:T(8,128)(2,1)S(1)} %pad_maximum_fusion.6), channel_id=1, source_target_pairs={{0,16},{1,17},{2,18},{3,19},{4,20},{5,21},{6,22},{7,23},{8,24},{9,... | collective-permute-start | bytes 393224 | tf_op jit(solution)/shard_map/ppermute | solution.py:522
  31.3 8.7 %collective-permute-start.11 = (bf16[2,64,512]{2,1,0:T(8,128)(2,1)S(1)}, bf16[2,64,512]{2,1,0:T(8,128)(2,1)S(1)}, u32[]{:S(2)}, u32[]{:S(2)}) collective-permute-start(bf16[2,64,512]{2,1,0:T(8,128)(2,1)S(1)} %pad_maximum_fusion.6), channel_id=1, source_target_pairs={{0,24},{1,25},{2,26},{3,27},{4,28},{5,29},{6,30},{7,31},{8,16},{9,... | collective-permute-start | bytes 393224 | tf_op jit(solution)/shard_map/ppermute | solution.py:522
  40.3 16.1 %collective-permute-start.12 = (bf16[4,9,64,128]{3,2,1,0:T(8,128)(2,1)S(1)}, bf16[4,9,64,128]{3,2,1,0:T(8,128)(2,1)S(1)}, u32[]{:S(2)}, u32[]{:S(2)}) collective-permute-start(bf16[4,9,64,128]{3,2,1,0:T(8,128)(2,1)S(1)} %collective-permute-done.7.refs_6_), channel_id=1, source_target_pairs={{0,2},{1,5},{2,0},{3,7},{4,6},{5,1},{6,4},{7,3},{8,10},{9,13},{10,... | collective-permute-start | bytes 1769480 | tf_op jit(solution)/shard_map/ppermute | solution.py:522
  40.9 15.5 %collective-permute-start.13 = (bf16[4,2,64,512]{3,2,1,0:T(8,128)(2,1)S(1)}, bf16[4,2,64,512]{3,2,1,0:T(8,128)(2,1)S(1)}, u32[]{:S(2)}, u32[]{:S(2)}) collective-permute-start(bf16[4,2,64,512]{3,2,1,0:T(8,128)(2,1)S(1)} %pad_maximum_fusion.2.refs_8_), channel_id=1, source_target_pairs={{0,4},{1,5},{2,6},{3,7},{4,0},{5,1},{6,2},{7,3},{8,12},{9,13},{10,... | collective-permute-start | bytes 1572872 | tf_op jit(solution)/shard_map/ppermute | solution.py:522
  44.5 11.9 %collective-permute-start.15 = (bf16[2,64,512]{2,1,0:T(8,128)(2,1)S(1)}, bf16[2,64,512]{2,1,0:T(8,128)(2,1)S(1)}, u32[]{:S(2)}, u32[]{:S(2)}) collective-permute-start(bf16[2,64,512]{2,1,0:T(8,128)(2,1)S(1)} %pad_maximum_fusion.5), channel_id=1, source_target_pairs={{0,16},{1,17},{2,18},{3,19},{4,20},{5,21},{6,22},{7,23},{8,24},{9,... | collective-permute-start | bytes 393224 | tf_op jit(solution)/shard_map/ppermute | solution.py:522
  45.7 10.7 %collective-permute-start.16 = (bf16[2,64,512]{2,1,0:T(8,128)(2,1)S(1)}, bf16[2,64,512]{2,1,0:T(8,128)(2,1)S(1)}, u32[]{:S(2)}, u32[]{:S(2)}) collective-permute-start(bf16[2,64,512]{2,1,0:T(8,128)(2,1)S(1)} %pad_maximum_fusion.5), channel_id=1, source_target_pairs={{0,24},{1,25},{2,26},{3,27},{4,28},{5,29},{6,30},{7,31},{8,16},{9,... | collective-permute-start | bytes 393224 | tf_op jit(solution)/shard_map/ppermute | solution.py:522
  59.3 16.4 %collective-permute-start.22 = (bf16[4,2,64,512]{3,2,1,0:T(8,128)(2,1)S(1)}, bf16[4,2,64,512]{3,2,1,0:T(8,128)(2,1)S(1)}, u32[]{:S(2)}, u32[]{:S(2)}) collective-permute-start(bf16[4,2,64,512]{3,2,1,0:T(8,128)(2,1)S(1)} %pad_maximum_fusion.3.refs_12_), channel_id=1, source_target_pairs={{0,4},{1,5},{2,6},{3,7},{4,0},{5,1},{6,2},{7,3},{8,12},{9,13},{10,... | collective-permute-start | bytes 1572872 | tf_op jit(solution)/shard_map/ppermute | solution.py:522
  60.9 14.8 %collective-permute-start.23 = (bf16[4,2,64,512]{3,2,1,0:T(8,128)(2,1)S(1)}, bf16[4,2,64,512]{3,2,1,0:T(8,128)(2,1)S(1)}, u32[]{:S(2)}, u32[]{:S(2)}) collective-permute-start(bf16[4,2,64,512]{3,2,1,0:T(8,128)(2,1)S(1)} %pad_maximum_fusion.3.refs_12_), channel_id=1, source_target_pairs={{0,1},{1,0},{2,3},{3,2},{4,5},{5,4},{6,7},{7,6},{8,9},{9,8},{10,11... | collective-permute-start | bytes 1572872 | tf_op jit(solution)/shard_map/ppermute | solution.py:522
  61.2 14.5 %collective-permute-start.21 = (bf16[4,2,64,512]{3,2,1,0:T(8,128)(2,1)S(1)}, bf16[4,2,64,512]{3,2,1,0:T(8,128)(2,1)S(1)}, u32[]{:S(2)}, u32[]{:S(2)}) collective-permute-start(bf16[4,2,64,512]{3,2,1,0:T(8,128)(2,1)S(1)} %pad_maximum_fusion.2.refs_8_), channel_id=1, source_target_pairs={{0,1},{1,0},{2,3},{3,2},{4,5},{5,4},{6,7},{7,6},{8,9},{9,8},{10,11... | collective-permute-start | bytes 1572872 | tf_op jit(solution)/shard_map/ppermute | solution.py:522
  62.1 9.1 %collective-permute-start.24 = (bf16[1024,128]{1,0:T(8,128)(2,1)S(1)}, bf16[1024,128]{1,0:T(8,128)(2,1)S(1)}, u32[]{:S(2)}, u32[]{:S(2)}) collective-permute-start(bf16[1024,128]{1,0:T(8,128)(2,1)S(1)} %get-tuple-element.294), channel_id=1, source_target_pairs={{0,2},{1,3},{2,0},{3,1},{4,6},{5,7},{6,4},{7,5},{8,10},{9,11},{10,... | collective-permute-start | bytes 786440 | tf_op jit(solution)/shard_map/ppermute | solution.py:599
  62.9 12.8 %collective-permute-start.25 = (bf16[1024,128]{1,0:T(8,128)(2,1)S(1)}, bf16[1024,128]{1,0:T(8,128)(2,1)S(1)}, u32[]{:S(2)}, u32[]{:S(2)}) collective-permute-start(bf16[1024,128]{1,0:T(8,128)(2,1)S(1)} %get-tuple-element.293), channel_id=1, source_target_pairs={{0,3},{1,2},{2,1},{3,0},{4,7},{5,6},{6,5},{7,4},{8,11},{9,10},{10,... | collective-permute-start | bytes 786440 | tf_op jit(solution)/shard_map/ppermute | solution.py:599
  101.4 14.8 %collective-permute-start.36 = (bf16[2,4,2,64,512]{4,3,2,1,0:T(8,128)(2,1)S(1)}, bf16[2,4,2,64,512]{4,3,2,1,0:T(8,128)(2,1)S(1)}, u32[]{:S(2)}, u32[]{:S(2)}) collective-permute-start(bf16[2,4,2,64,512]{4,3,2,1,0:T(8,128)(2,1)S(1)} %fusion), channel_id=1, source_target_pairs={{0,2},{1,5},{2,0},{3,7},{4,6},{5,1},{6,4},{7,3},{8,10},{9,13},{10,... | collective-permute-start | bytes 3145736 | tf_op jit(solution)/shard_map/ppermute | solution.py:522
  117.5 21.7 %collective-permute-start.37 = (bf16[2,4,9,64,128]{4,3,2,1,0:T(8,128)(2,1)S(1)}, bf16[2,4,9,64,128]{4,3,2,1,0:T(8,128)(2,1)S(1)}, u32[]{:S(2)}, u32[]{:S(2)}) collective-permute-start(bf16[2,4,9,64,128]{4,3,2,1,0:T(8,128)(2,1)S(1)} %get-tuple-element.240), channel_id=1, source_target_pairs={{0,2},{1,5},{2,0},{3,7},{4,6},{5,1},{6,4},{7,3},{8,10},{9,13},{10,... | collective-permute-start | bytes 3538952 | tf_op jit(solution)/shard_map/ppermute | solution.py:522
  118.1 21.9 %collective-permute-start.45 = (bf16[4,2,64,512]{3,2,1,0:T(8,128)(2,1)S(1)}, bf16[4,2,64,512]{3,2,1,0:T(8,128)(2,1)S(1)}, u32[]{:S(2)}, u32[]{:S(2)}) collective-permute-start(bf16[4,2,64,512]{3,2,1,0:T(8,128)(2,1)S(1)} %fusion.1), channel_id=1, source_target_pairs={{0,4},{1,3},{2,6},{3,1},{4,0},{5,7},{6,2},{7,5},{8,12},{9,11},{10,... | collective-permute-start | bytes 1572872 | tf_op jit(solution)/shard_map/ppermute | solution.py:522
  139.5 12.2 %collective-permute-start.38 = (bf16[4,9,64,128]{3,2,1,0:T(8,128)(2,1)S(1)}, bf16[4,9,64,128]{3,2,1,0:T(8,128)(2,1)S(1)}, u32[]{:S(2)}, u32[]{:S(2)}) collective-permute-start(bf16[4,9,64,128]{3,2,1,0:T(8,128)(2,1)S(1)} %fusion.2), channel_id=1, source_target_pairs={{0,4},{1,3},{2,6},{3,1},{4,0},{5,7},{6,2},{7,5},{8,12},{9,11},{10,... | collective-permute-start | bytes 1769480 | tf_op jit(solution)/shard_map/ppermute | solution.py:522
  140.1 13.0 %collective-permute-start.42 = (bf16[1024,128]{1,0:T(8,128)(2,1)S(1)}, bf16[1024,128]{1,0:T(8,128)(2,1)S(1)}, u32[]{:S(2)}, u32[]{:S(2)}) collective-permute-start(bf16[1024,128]{1,0:T(8,128)(2,1)S(1)} %get-tuple-element.245), channel_id=1, source_target_pairs={{0,1},{1,0},{2,3},{3,2},{4,5},{5,4},{6,7},{7,6},{8,9},{9,8},{10,11... | collective-permute-start | bytes 786440 | tf_op jit(solution)/shard_map/ppermute | solution.py:723
  140.3 15.3 %collective-permute-start.46 = (bf16[2,64,512]{2,1,0:T(8,128)(2,1)S(1)}, bf16[2,64,512]{2,1,0:T(8,128)(2,1)S(1)}, u32[]{:S(2)}, u32[]{:S(2)}) collective-permute-start(bf16[2,64,512]{2,1,0:T(8,128)(2,1)S(1)} %get-tuple-element.278), channel_id=1, source_target_pairs={{0,8},{1,9},{2,10},{3,11},{4,12},{5,13},{6,14},{7,15},{8,0},{9,1},... | collective-permute-start | bytes 393224 | tf_op jit(solution)/shard_map/ppermute | solution.py:522
  149.2 12.9 %collective-permute-start.47 = (bf16[2,64,512]{2,1,0:T(8,128)(2,1)S(1)}, bf16[2,64,512]{2,1,0:T(8,128)(2,1)S(1)}, u32[]{:S(2)}, u32[]{:S(2)}) collective-permute-start(bf16[2,64,512]{2,1,0:T(8,128)(2,1)S(1)} %get-tuple-element.280), channel_id=1, source_target_pairs={{0,16},{1,17},{2,18},{3,19},{4,20},{5,21},{6,22},{7,23},{8,24},{9,... | collective-permute-start | bytes 393224 | tf_op jit(solution)/shard_map/ppermute | solution.py:522
  151.1 11.1 %collective-permute-start.48 = (bf16[2,64,512]{2,1,0:T(8,128)(2,1)S(1)}, bf16[2,64,512]{2,1,0:T(8,128)(2,1)S(1)}, u32[]{:S(2)}, u32[]{:S(2)}) collective-permute-start(bf16[2,64,512]{2,1,0:T(8,128)(2,1)S(1)} %get-tuple-element.279), channel_id=1, source_target_pairs={{0,24},{1,25},{2,26},{3,27},{4,28},{5,29},{6,30},{7,31},{8,16},{9,... | collective-permute-start | bytes 393224 | tf_op jit(solution)/shard_map/ppermute | solution.py:522
  151.7 23.6 %collective-permute-start.43 = (bf16[1024,128]{1,0:T(8,128)(2,1)S(1)}, bf16[1024,128]{1,0:T(8,128)(2,1)S(1)}, u32[]{:S(2)}, u32[]{:S(2)}) collective-permute-start(bf16[1024,128]{1,0:T(8,128)(2,1)S(1)} %get-tuple-element.246), channel_id=1, source_target_pairs={{0,2},{1,3},{2,0},{3,1},{4,6},{5,7},{6,4},{7,5},{8,10},{9,11},{10,... | collective-permute-start | bytes 786440 | tf_op jit(solution)/shard_map/ppermute | solution.py:723
  153.1 22.2 %collective-permute-start.44 = (bf16[1024,128]{1,0:T(8,128)(2,1)S(1)}, bf16[1024,128]{1,0:T(8,128)(2,1)S(1)}, u32[]{:S(2)}, u32[]{:S(2)}) collective-permute-start(bf16[1024,128]{1,0:T(8,128)(2,1)S(1)} %get-tuple-element.247), channel_id=1, source_target_pairs={{0,3},{1,2},{2,1},{3,0},{4,7},{5,6},{6,5},{7,4},{8,11},{9,10},{10,... | collective-permute-start | bytes 786440 | tf_op jit(solution)/shard_map/ppermute | solution.py:723
  155.6 10.6 %collective-permute-start.39 = (bf16[9,64,128]{2,1,0:T(8,128)(2,1)S(1)}, bf16[9,64,128]{2,1,0:T(8,128)(2,1)S(1)}, u32[]{:S(2)}, u32[]{:S(2)}) collective-permute-start(bf16[9,64,128]{2,1,0:T(8,128)(2,1)S(1)} %get-tuple-element.283), channel_id=1, source_target_pairs={{0,8},{1,9},{2,10},{3,11},{4,12},{5,13},{6,14},{7,15},{8,0},{9,1},... | collective-permute-start | bytes 442376 | tf_op jit(solution)/shard_map/ppermute | solution.py:522
  162.2 13.1 %collective-permute-start.40 = (bf16[9,64,128]{2,1,0:T(8,128)(2,1)S(1)}, bf16[9,64,128]{2,1,0:T(8,128)(2,1)S(1)}, u32[]{:S(2)}, u32[]{:S(2)}) collective-permute-start(bf16[9,64,128]{2,1,0:T(8,128)(2,1)S(1)} %get-tuple-element.282), channel_id=1, source_target_pairs={{0,16},{1,17},{2,18},{3,19},{4,20},{5,21},{6,22},{7,23},{8,24},{9,... | collective-permute-start | bytes 442376 | tf_op jit(solution)/shard_map/ppermute | solution.py:522
  162.2 13.1 %collective-permute-start.41 = (bf16[9,64,128]{2,1,0:T(8,128)(2,1)S(1)}, bf16[9,64,128]{2,1,0:T(8,128)(2,1)S(1)}, u32[]{:S(2)}, u32[]{:S(2)}) collective-permute-start(bf16[9,64,128]{2,1,0:T(8,128)(2,1)S(1)} %get-tuple-element.281), channel_id=1, source_target_pairs={{0,24},{1,25},{2,26},{3,27},{4,28},{5,29},{6,30},{7,31},{8,16},{9,... | collective-permute-start | bytes 442376 | tf_op jit(solution)/shard_map/ppermute | solution.py:522
  (39 other events, 281.7 us)
